TPU v7x, 512 devices: a whole 4x8x8 slice. The times are simulated.
512 devices in a mesh: leaf: 32 (over y_lo, z, core), row: 4 (over x), col: 4 (over y_hi).
Axes of the slice: x: 4, y: 8 (y_hi: 4, y_lo: 2; y = y_hi * 2 + y_lo), z: 8, core: 2. Of those that a mesh axis runs over, the one named last changes fastest.
Arguments:
- panel: float32 [131072, 1024], P(('leaf', 'row'), 'col'), may hold values from -1.2 to 1.2
- block_mask: int32 [1024, 8], P(('leaf', 'row'), 'col'), may hold values 0 or 1
- front_rest: float32 [65536, 4096], P(('leaf', 'row'), 'col'), may hold values from -6 to 6
- row_maps: int32 [128, 4], P(('leaf', 'row')), may hold values from 0 to 3, each once within a row
- col_maps: int32 [128, 12], P(('leaf', 'col')), may hold values from 0 to 11, each once within a row
Outputs:
- parent: float32 [32768, 6144], P(('leaf', 'row'), 'col')
Inputs may be any that keep to these rules, and one draw needn't show every extreme that they name: `row_maps`: each row is a permutation of 0 to 3. `col_maps`: each row is a permutation of 0 to 11; only its first 8 entries are used.
All inputs are finite; a program needn't handle non-finite values. No bound on the sum of `block_mask` on one device may be relied on, other than what follows from the above.
Results may differ from a plain program's by a relative error of at most 0.0003.
Values sent between devices are 32-bit elements; how exact they have to be, the bound alone decides.
No kernel may reach another device: no remote copies, remote signals or barrier semaphores. Data moves between devices by JAX's collectives and lax.ppermute only.
A program may use at most 64 MiB of HBM per device.

v0:
```python
import jax
import jax.numpy as jnp
from jax import lax
from jax.sharding import PartitionSpec as P

BLK = 128
PC = 6144


def spread(value, axis, root):
    mine = lax.axis_index(axis) == root
    return lax.psum(jnp.where(mine, value, jnp.zeros_like(value)), axis)


def partner(value, axis, stride):
    mask = 2**stride
    pairs = [(source, source ^ mask) for source in range(lax.axis_size(axis))]
    return lax.ppermute(value, axis, pairs)


def spread_blocks(values, rows_at, cols_at, count, parent_blocks):
    empty = jnp.zeros((count, parent_blocks, BLK, BLK), jnp.float32)
    return empty.at[rows_at[:, None], cols_at[None, :]].add(values)


def as_blocks(update_rows):
    count = update_rows.shape[0] // BLK
    columns = update_rows.shape[1] // BLK
    return update_rows.reshape(count, BLK, columns, BLK).transpose(0, 2, 1, 3)


def body(panel, block_mask, front_rest, row_maps, col_maps):
    local_rows, local_width = panel.shape
    flags = block_mask.astype(jnp.float32)
    masked = (
        panel.reshape(local_rows // BLK, BLK, local_width // BLK, BLK) * flags[:, None, :, None]
    ).reshape(local_rows, local_width)
    win_rows = front_rest.shape[0]
    window = masked[:win_rows]
    own_rows = lax.all_gather(masked, "col", axis=1, tiled=True)
    columns = spread(own_rows, "row", lax.axis_index("col"))
    product = lax.dot_general(
        lax.all_gather(window, "col", axis=1, tiled=True),
        columns,
        (((1,), (1,)), ((), ())),
        precision=lax.Precision.HIGHEST,
        preferred_element_type=jnp.float32,
    )
    update = front_rest - product
    win_blocks = win_rows // BLK
    child_blocks = update.shape[1] // BLK
    parent_blocks = PC // (BLK * lax.axis_size("col"))
    keep_count = win_blocks // 2
    shift_bit = lax.axis_size("leaf").bit_length() - 2
    upper = lax.axis_index("leaf") // (lax.axis_size("leaf") // 2) % 2
    base = upper * keep_count
    row_targets = row_maps[0]
    col_targets = col_maps[0, :child_blocks]
    other_update, other_rows, other_cols = partner((update, row_maps, col_maps), "leaf", shift_bit)
    mine = spread_blocks(as_blocks(update), row_targets, col_targets, win_blocks, parent_blocks)
    mine = mine + spread_blocks(
        as_blocks(other_update),
        other_rows[0],
        other_cols[0, :child_blocks],
        win_blocks,
        parent_blocks,
    )
    kept = lax.dynamic_slice_in_dim(mine, base, keep_count, 0)
    return kept.transpose(0, 2, 1, 3).reshape(keep_count * BLK, parent_blocks * BLK)


def solution(mesh):
    return jax.shard_map(
        body,
        mesh=mesh,
        in_specs=(
            P(("leaf", "row"), "col"),
            P(("leaf", "row"), "col"),
            P(("leaf", "row"), "col"),
            P(("leaf", "row"), None),
            P(("leaf", "col"), None),
        ),
        out_specs=P(("leaf", "row"), "col"),
        check_vma=False,
    )
```

profile of v0, /device:TPU:448, one launch (start us, length us, event | category | flops | bytes accessed | tf_op | source)
XLA Modules:
  0.0 338.0 jit_solution(4224685826812037165)
XLA Ops:
  6.5 0.0 all-gather.5.cloned.1.call-start
  6.5 0.7 convert_element_type.3
  7.2 0.1 copy.7
  7.3 0.0 copy-start.3
  7.3 0.3 mul.16
  7.6 0.0 copy-start.1
  7.7 2.4 bitcast_multiply_fusion
  10.1 0.0 all-gather.5.cloned.1.call-update
  10.1 0.0 all-gather.3.cloned.1.call-start
  10.1 0.0 copy-done.3
  10.2 0.0 copy-done.1
  10.2 0.0 slice-start
  10.2 0.5 reshape.72
  10.7 0.1 slice-done
  10.8 0.2 slice_multiply_fusion
  11.1 0.8 copy.23
  11.9 0.0 all-gather.3.cloned.1.call-update
  12.0 0.0 all-reduce.2.cloned.1.call-start
  12.0 86.0 %all-gather.5.cloned.1.call-done = f32[1024,1024]{1,0:T(8,128)} async-done(((f32[1024,256]{1,0:T(8,128)}), f32[1024,1024]{1,0:T(8,128)}) %all-gather.5.cloned.1.call-update) | async-done | bytes 4194320 | tf_op jit(solution)/shard_map/all_gather | solution.py:40
  98.0 5.0 %broadcast_select_fusion = f32[1024,1024]{1,0:T(8,128)} fusion(f32[1024,1024]{1,0:T(8,128)} %all-gather.5.cloned.1.call-done, pred[]{:T(512)S(6)} %eq.5), kind=kLoop, calls=%fused_computation.2 | loop fusion | flops 1048576 | bytes 8388609 | tf_op jit(solution)/shard_map/jit(_where)/select_n | solution.py:12
  103.0 0.0 copy-start.4
  103.0 0.0 copy-start.5
  103.0 0.0 copy-start.2
  103.0 0.0 all-reduce.2.cloned.1.call-update
  103.0 0.6 copy-done.4
  103.7 2.7 collective-permute-start
  106.4 0.0 copy-done.5
  106.4 3.3 collective-permute-start.1
  109.6 39.6 %all-gather.3.cloned.1.call-done = f32[512,1024]{1,0:T(8,128)} async-done(((f32[512,256]{1,0:T(8,128)}), f32[512,1024]{1,0:T(8,128)}) %all-gather.3.cloned.1.call-update) | async-done | bytes 2097168 | tf_op jit(solution)/shard_map/all_gather | solution.py:43
  149.2 108.7 %all-reduce.2.cloned.1.call-done = f32[1024,1024]{1,0:T(8,128)} async-done(((f32[1024,1024]{1,0:T(8,128)}), f32[1024,1024]{1,0:T(8,128)}) %all-reduce.2.cloned.1.call-update) | async-done | bytes 4194320 | tf_op jit(solution)/shard_map/psum | solution.py:12
  257.9 0.0 copy-done.2
  257.9 10.3 %convolution_subtract_fusion = f32[512,1024]{1,0:T(8,128)} fusion(f32[512,1024]{1,0:T(8,128)S(1)} %copy-done.2, f32[512,1024]{1,0:T(8,128)} %all-gather.3.cloned.1.call-done, f32[1024,1024]{1,0:T(8,128)} %all-reduce.2.cloned.1.call-done), kind=kOutput, calls=%fused_computation.6 | convolution fusion | flops 6442975232 | bytes 10485760 | tf_op jit(solution)/shard_map/dot_general | solution.py:42
  268.2 3.6 %collective-permute-start.2 = (f32[512,1024]{1,0:T(8,128)}, f32[512,1024]{1,0:T(8,128)}, u32[]{:S(2)}, u32[]{:S(2)}) collective-permute-start(f32[512,1024]{1,0:T(8,128)} %convolution_subtract_fusion), channel_id=1, source_target_pairs={{0,256},{16,272},{32,288},{48,304},{64,320},{80,336},{96,352},{112... | collective-permute-start | bytes 6291464 | tf_op jit(solution)/shard_map/ppermute | solution.py:18
  271.9 0.1 or_select_fusion.1
  272.0 0.1 reshape.76
  272.0 0.0 collective-permute-done
  272.1 0.0 collective-permute-done.1
  272.1 0.1 or_select_fusion
  272.2 0.1 reshape.82
  272.3 2.1 copy.16
  274.3 1.7 copy.8
  276.0 0.4 broadcast.45.clone.1
  276.4 5.2 %scatter_fusion = f32[4,12,128,128]{3,2,1,0:T(8,128)S(1)} fusion(f32[4,12,128,128]{3,2,1,0:T(8,128)S(1)} %broadcast.45.clone.1, s32[32]{0:T(128)S(1)} %reshape.76, f32[32,128,128]{2,1,0:T(8,128)} %bitcast.59), kind=kCustom, calls=%fused_computation | custom fusion | flops 524288 | bytes 6291712 | tf_op jit(solution)/shard_map/scatter-add | solution.py:23
  281.6 0.0 copy-start
  281.6 36.2 %collective-permute-done.2 = f32[512,1024]{1,0:T(8,128)} collective-permute-done((f32[512,1024]{1,0:T(8,128)}, f32[512,1024]{1,0:T(8,128)}, u32[]{:S(2)}, u32[]{:S(2)}) %collective-permute-start.2) | collective-permute-done | bytes 2097184 | tf_op jit(solution)/shard_map/ppermute | solution.py:18
  317.8 2.1 copy.17
  319.8 0.0 copy-done
  319.9 1.7 copy.9
  321.6 0.4 broadcast.45.clone
  321.9 5.2 %scatter_fusion.1 = f32[4,12,128,128]{3,2,1,0:T(8,128)S(1)} fusion(f32[4,12,128,128]{3,2,1,0:T(8,128)S(1)} %broadcast.45.clone, s32[32]{0:T(128)S(1)} %reshape.82, f32[32,128,128]{2,1,0:T(8,128)} %bitcast.58), kind=kCustom, calls=%fused_computation.1 | custom fusion | flops 524288 | bytes 6291712 | tf_op jit(solution)/shard_map/scatter-add | solution.py:23
  327.2 1.6 fusion
  328.7 0.9 copy.12
  329.7 1.8 copy.22
  (8 shorter events, 0.1 us)
Async XLA Ops:
  6.5 91.5 %all-gather.5.cloned.1.call-start = ((), (), s32[]{:S(2)}) async-start(), calls=%async_computation.1 | async-start | bytes 5242880 | tf_op jit(solution)/shard_map/all_gather | solution.py:40
  7.3 2.8 copy-start.3
  7.6 2.5 copy-start.1
  10.1 139.1 %all-gather.3.cloned.1.call-start = ((), (), s32[]{:S(2)}) async-start(), calls=%async_computation | async-start | bytes 2621440 | tf_op jit(solution)/shard_map/all_gather | solution.py:43
  10.2 0.7 slice-start
  12.0 246.0 %all-reduce.2.cloned.1.call-start = ((), (), s32[]{:S(2)}) async-start(), calls=%async_computation.2 | async-start | bytes 8388608 | tf_op jit(solution)/shard_map/psum | solution.py:12
  103.0 0.7 copy-start.4
  103.0 3.4 copy-start.5
  103.0 154.9 %copy-start.2 = (f32[512,1024]{1,0:T(8,128)S(1)}, f32[512,1024]{1,0:T(8,128)}, u32[]{:S(2)}) copy-start(f32[512,1024]{1,0:T(8,128)} %param.7) | copy-start | bytes 6291460
  103.7 168.4 %collective-permute-start = (s32[1,4]{1,0:T(1,128)S(1)}, s32[1,4]{1,0:T(1,128)S(1)}, u32[]{:S(2)}, u32[]{:S(2)}) collective-permute-start(s32[1,4]{1,0:T(1,128)S(1)} %copy-done.4), channel_id=1, source_target_pairs={{0,256},{16,272},{32,288},{48,304},{64,320},{80,336},{96,352},{112... | collective-permute-start | bytes 56 | tf_op jit(solution)/shard_map/ppermute | solution.py:18
  106.4 165.7 %collective-permute-start.1 = (s32[1,12]{1,0:T(1,128)S(1)}, s32[1,12]{1,0:T(1,128)S(1)}, u32[]{:S(2)}, u32[]{:S(2)}) collective-permute-start(s32[1,12]{1,0:T(1,128)S(1)} %copy-done.5), channel_id=1, source_target_pairs={{0,256},{16,272},{32,288},{48,304},{64,320},{80,336},{96,352},{112... | collective-permute-start | bytes 152 | tf_op jit(solution)/shard_map/ppermute | solution.py:18
  268.2 49.6 %collective-permute-start.2 = (f32[512,1024]{1,0:T(8,128)}, f32[512,1024]{1,0:T(8,128)}, u32[]{:S(2)}, u32[]{:S(2)}) collective-permute-start(f32[512,1024]{1,0:T(8,128)} %convolution_subtract_fusion), channel_id=1, source_target_pairs={{0,256},{16,272},{32,288},{48,304},{64,320},{80,336},{96,352},{112... | collective-permute-start | bytes 6291464 | tf_op jit(solution)/shard_map/ppermute | solution.py:18
  281.6 38.2 %copy-start = (f32[4,12,128,128]{3,2,1,0:T(8,128)}, f32[4,12,128,128]{3,2,1,0:T(8,128)S(1)}, u32[]{:S(2)}) copy-start(f32[4,12,128,128]{3,2,1,0:T(8,128)S(1)} %scatter_fusion) | copy-start | bytes 9437188
Sparse Core Ops, SparseCore 0:
  10.2 87.7 all-gather.4
  100.1 49.0 all-gather.2
  151.6 106.3 all-reduce.1
where the time goes:
time: 344 us; the launch traced here: 338 us
  waiting for transfers between devices  271 us (79%)
  other arithmetic  20.5 us (6%)
  local copies, waits for them, and re-layouts  13.7 us (4%)
  between operations  13.4 us (4%)
  matrix products  10.3 us (3%)
  starting transfers between devices  9.61 us (3%)
    psum x1, waiting for transfers between devices, spread(): return lax.psum(jnp.where(mine, value, jnp.zeros_like(value)), axis)  109 us
    all_gather x1, waiting for transfers between devices, body(): own_rows = lax.all_gather(masked, 'col', axis=1, tiled=True)  86 us
    all_gather x1, waiting for transfers between devices, body(): lax.all_gather(window, 'col', axis=1, tiled=True)  39.6 us
    ppermute x3, waiting for transfers between devices, partner(): return lax.ppermute(value, axis, pairs)  36.2 us
    scatter-add x2, other arithmetic, spread_blocks(): return empty.at[rows_at[:, None], cols_at[None, :]].add(values)  10.4 us
    dot_general x1, matrix products, body(): lax.dot_general(lax.all_gather(window, 'col', axis=1, tiled=True), column...  10.3 us
    ppermute x3, starting transfers between devices, partner(): return lax.ppermute(value, axis, pairs)  9.53 us
    unnamed x16, local copies, waits for them, and re-layouts  7.41 us
  transfers between devices with their start and end apart: 6, of which 4 were waited for; matrix products, arithmetic and copies ran while one was open for 8% of the time, Pallas kernels for 0%

commit v1 on v0

v1 whole, which is shorter than its diff:
```python
import functools

import jax
import jax.numpy as jnp
from jax import lax
from jax.experimental import pallas as pl
from jax.experimental.pallas import tpu as pltpu
from jax.sharding import PartitionSpec as P

BLK = 128
PC = 6144
F32 = jnp.float32
BF16 = jnp.bfloat16
VMEM = pl.BlockSpec(memory_space=pltpu.VMEM)
ANY = pl.BlockSpec(memory_space=pl.ANY)
SMEM = pl.BlockSpec(memory_space=pltpu.SMEM)
LIMIT = 16 * 1024 * 1024


def cost(us):
    return pl.CostEstimate(flops=int(us * 1e9), bytes_accessed=int(us * 2e6), transcendentals=0)


def shift(value, axis, by):
    size = lax.axis_size(axis)
    return lax.ppermute(value, axis, [(i, (i + by) % size) for i in range(size)])


def mask_kernel(flags_ref, panel_ref, out_ref, window_ref):
    for i in range(out_ref.shape[0] // BLK):
        for k in range(out_ref.shape[1] // BLK):
            rows, columns = pl.ds(i * BLK, BLK), pl.ds(k * BLK, BLK)
            value = panel_ref[rows, columns] * flags_ref[k, i].astype(F32)
            out_ref[rows, columns] = value
            if i * BLK < window_ref.shape[0]:
                window_ref[rows, columns] = value


def mask_rows(block_mask, panel, win_rows):
    half = jax.ShapeDtypeStruct((win_rows, panel.shape[1]), F32)
    return pl.pallas_call(
        mask_kernel,
        out_shape=[jax.ShapeDtypeStruct(panel.shape, F32), half],
        in_specs=[SMEM, VMEM],
        out_specs=[VMEM] * 2,
        compiler_params=pltpu.CompilerParams(vmem_limit_bytes=LIMIT),
        cost_estimate=cost(1.5),
    )(block_mask.T, panel)


def after_all(value, *others):
    return lax.optimization_barrier((value, *others))[0]


def halves(value):
    high = value.astype(BF16)
    return high, (value - high.astype(F32)).astype(BF16)


def window_kernel(groups, to_ref, *refs):
    pieces, (high_ref, low_ref) = refs[:-2], refs[-2:]
    for d in range(groups):
        per = len(pieces) // groups
        j = 0
        for piece in pieces[d * per : (d + 1) * per]:
            for i in range(piece.shape[0] // BLK):
                at = pl.ds(pl.multiple_of(to_ref[j] * BLK, BLK), BLK)
                high_ref[d, at], low_ref[d, at] = halves(piece[pl.ds(i * BLK, BLK)])
                j += 1


def split_window(to, groups, *pieces):
    rows = sum(p.shape[0] for p in pieces) // groups
    out = jax.ShapeDtypeStruct((groups, rows, pieces[0].shape[1]), BF16)
    return pl.pallas_call(
        functools.partial(window_kernel, groups),
        out_shape=[out, out],
        in_specs=[SMEM] + [VMEM] * len(pieces),
        out_specs=[VMEM, VMEM],
        compiler_params=pltpu.CompilerParams(vmem_limit_bytes=LIMIT),
        cost_estimate=cost(0.4 * groups),
    )(to, *pieces)


def update_kernel(counts, firsts, quarter_ref, from_ref, place_ref, near_high, near_low, far_high, far_low, front_ref, *refs):
    (big_ref, small_ref), refs = refs[-2:], refs[:-2]
    pieces, outs = refs[: sum(map(len, counts))], refs[sum(map(len, counts)) :]
    rows, width = outs[0].shape[0], outs[0].shape[1] // len(counts)
    first, span = firsts[0] * BLK, rows * len(outs)
    near = near_high.shape[0]
    for q, parts in enumerate(counts):
        k = 0
        for count in parts:
            piece, pieces = pieces[0], pieces[1:]
            for i in range(count):
                big_ref[q, k], small_ref[q, k] = halves(piece[i])
                k += 1
        total = None
        for d in range(near + 1):
            high, low, e = (near_high, near_low, d) if d < near else (far_high, far_low, 0)
            ph, plo = big_ref[q, place_ref[d]], small_ref[q, place_ref[d]]
            for left, right in ((high, ph), (high, plo), (low, ph)):
                term = lax.dot_general(
                    left[e, pl.ds(first, span)], right, (((1,), (1,)), ((), ())), preferred_element_type=F32
                )
                total = term if total is None else total + term
        columns = pl.ds(pl.multiple_of(quarter_ref[q] * width, width), width)
        for o, out_ref in enumerate(outs):
            for i in range(rows // BLK):
                source = pl.ds(pl.multiple_of(from_ref[firsts[o] + i] * BLK, BLK), BLK)
                at = o * rows + i * BLK
                out_ref[pl.ds(i * BLK, BLK), pl.ds(q * width, width)] = (
                    front_ref[source, columns] - total[at : at + BLK]
                )


def update(quarters, sources, place, window, front, groups, firsts, us):
    counts = tuple(tuple(p.shape[0] for p in group) for group in groups)
    pieces = [p for group in groups for p in group]
    out = jax.ShapeDtypeStruct((front.shape[0] // 2, len(groups) * pieces[0].shape[1]), F32)
    return pl.pallas_call(
        functools.partial(update_kernel, counts, firsts),
        out_shape=[out] * len(firsts),
        in_specs=[SMEM] * 3 + [VMEM] * (5 + len(pieces)),
        out_specs=[VMEM] * len(firsts),
        scratch_shapes=[pltpu.VMEM((len(groups), sum(counts[0]), *pieces[0].shape[1:]), BF16)] * 2,
        compiler_params=pltpu.CompilerParams(vmem_limit_bytes=LIMIT),
        cost_estimate=cost(us),
    )(quarters, sources, place, *window, front, *pieces)


def place_kernel(count, mine_ref, other_ref, *refs):
    values, out_ref = refs[:-1], refs[-1]
    out_ref[...] = jnp.zeros_like(out_ref)
    for i, value_ref in enumerate(values):
        maps_ref = mine_ref if i < count else other_ref
        start = sum(v.shape[1] for v in values[:i]) if i < count else sum(v.shape[1] for v in values[count:i])
        for j in range(value_ref.shape[1] // BLK):
            at = pl.ds(pl.multiple_of(maps_ref[start // BLK + j] * BLK, BLK), BLK)
            value = value_ref[:, j * BLK : (j + 1) * BLK]
            out_ref[:, at] = value if i < count else out_ref[:, at] + value


def place_blocks(mine, other, own, got, columns):
    return pl.pallas_call(
        functools.partial(place_kernel, len(own)),
        out_shape=jax.ShapeDtypeStruct((own[0].shape[0], columns), F32),
        in_specs=[SMEM] * 2 + [VMEM] * (len(own) + len(got)),
        out_specs=VMEM,
        compiler_params=pltpu.CompilerParams(vmem_limit_bytes=LIMIT),
        cost_estimate=cost(2),
    )(mine, other, *own, *got)


def add_kernel(slots_ref, value_ref, sum_ref, out_ref):
    out_ref[...] = sum_ref[...] + value_ref[...]


def add_blocks(slots, value, total):
    rows = value.shape[0]
    placed = pl.BlockSpec((rows, BLK), lambda i, s: (0, s[i]))
    return pl.pallas_call(
        add_kernel,
        grid_spec=pltpu.PrefetchScalarGridSpec(
            num_scalar_prefetch=1,
            grid=(value.shape[1] // BLK,),
            in_specs=[pl.BlockSpec((rows, BLK), lambda i, s: (0, i)), placed],
            out_specs=placed,
        ),
        out_shape=jax.ShapeDtypeStruct(total.shape, F32),
        input_output_aliases={2: 0},
        compiler_params=pltpu.CompilerParams(vmem_limit_bytes=LIMIT),
        cost_estimate=cost(1),
    )(slots, value, total)


def body(panel, block_mask, front_rest, row_maps, col_maps):
    n_leaf, n_row, n_col = (lax.axis_size(a) for a in ("leaf", "row", "col"))
    row, col = lax.axis_index("row"), lax.axis_index("col")
    upper = lax.axis_index("leaf") // (n_leaf // 2) % 2
    win_rows, width = front_rest.shape[0], panel.shape[1]
    columns = panel.shape[0] // n_row
    pairs = [(i, i ^ (n_leaf // 2)) for i in range(n_leaf)]
    to_sibling = lambda v: lax.ppermute(v, "leaf", pairs)

    masked, window = mask_rows(block_mask, panel, win_rows)
    other_maps = to_sibling(col_maps)
    by_row = lax.all_to_all(masked, "row", 0, 0, tiled=True)
    by_row = after_all(by_row, other_maps)
    mine = lax.all_to_all(by_row, "col", 0, 0, tiled=True).reshape(n_col, columns, width)
    half = win_rows // 2
    before, after = shift(window, "col", 1), shift(window, "col", -1)
    far_low, far_high = shift(before[:half], "col", 1), shift(after[half:], "col", -1)
    q_before, q_after = shift(mine, "row", 1), shift(mine, "row", -1)
    q_low, q_high = shift(q_before[: n_col // 2], "row", 1), shift(q_after[n_col // 2 :], "row", -1)

    target = row_maps[0]
    to = jnp.where(target // 2 == upper, target % 2, 2 + target % 2).astype(jnp.int32)
    sources = jnp.sum(
        jnp.where(to[None, :] == jnp.arange(to.shape[0])[:, None], jnp.arange(to.shape[0])[None, :], 0), 1
    ).astype(jnp.int32)
    place = jnp.stack([col, (col + n_col - 1) % n_col, (col + 1) % n_col, (col + 2) % n_col]).astype(jnp.int32)
    window = (*split_window(to, 3, window, before, after), *split_window(after_all(to, q_before, q_after), 1, far_low, far_high))

    quarters = jnp.stack([row, (row + n_row - 1) % n_row, (row + 1) % n_row, (row + 2) % n_row]).astype(jnp.int32)
    half = win_rows // BLK // 2
    keep0, send0 = update(quarters[:1], sources, place, window, front_rest, ((mine,),), (0, half), 1.6)
    got0 = to_sibling(send0)
    keep1, send1 = update(quarters[1:3], sources, place, window, front_rest, ((q_before,), (q_after,)), (0, half), 3.2)
    got1 = to_sibling(send1)
    last = ((q_low, q_high),)
    (send2,) = update(quarters[3:], sources, place, window, front_rest, last, (half,), 1)
    got2 = to_sibling(send2)
    (keep2,) = update(quarters[3:], sources, place, window, front_rest, last, (0,), 1)

    per = columns // BLK
    order = (quarters[:, None] * per + jnp.arange(per)[None, :]).reshape(-1)
    pick = (order[:, None] == jnp.arange(n_row * per)[None, :]).astype(jnp.int32)
    slots, other_slots = (jnp.sum(pick * m[:, : n_row * per], 1) for m in (col_maps, other_maps))
    total = place_blocks(slots, other_slots, (keep0, keep1, keep2), (got0, got1), PC // n_col)
    return add_blocks(other_slots[3 * per :], got2, total)


def solution(mesh):
    return jax.shard_map(
        body,
        mesh=mesh,
        in_specs=(
            P(("leaf", "row"), "col"),
            P(("leaf", "row"), "col"),
            P(("leaf", "row"), "col"),
            P(("leaf", "row"), None),
            P(("leaf", "col"), None),
        ),
        out_specs=P(("leaf", "row"), "col"),
        check_vma=False,
    )
```

time: 344 us -> 133 us (0.39); the launches traced: 338 us -> 132 us
  waiting for transfers between devices: 271 us -> 59.3 us
  starting transfers between devices: 9.61 us -> 50 us
  other arithmetic: 20.5 us -> 0.63 us
  Pallas kernels: 0 us -> 15.9 us
  between operations: 13.4 us -> 0.34 us
  matrix products: 10.3 us -> 0 us
  local copies, waits for them, and re-layouts: 13.7 us -> 5.48 us
    all_gather x2 -> x0, waiting for transfers between devices: 126 us -> none  [the longest x1 86 us: body(): own_rows = lax.all_gather(masked, 'col', axis=1, tiled=True)]
    psum x1 -> x0, waiting for transfers between devices: 109 us -> none  [spread(): return lax.psum(jnp.where(mine, value, jnp.zeros_like(value)), axis)]
    all_to_all x0 -> x2, waiting for transfers between devices: none -> 38 us  [the longest x1 28.2 us: body(): lax.all_to_all(by_row, 'col', 0, 0, tiled=True)]
    ppermute x3 -> x12, starting transfers between devices: 9.53 us -> 38.5 us  [the longest x8 27.2 us: shift(): lax.ppermute(value, axis, [(i, (i + by) % size) for i in range(size)])]
    pallas_call x0 -> x9, Pallas kernels: none -> 15.9 us  [the longest x4 7.26 us: update(): pl.pallas_call(functools.partial(update_kernel, counts, firsts), out_shap...]
    ppermute x3 -> x12, waiting for transfers between devices: 36.2 us -> 21.3 us  [the longest x4 11 us: body(): to_sibling = lambda v: lax.ppermute(v, 'leaf', pairs)]
    all_to_all x0 -> x2, starting transfers between devices: none -> 11.5 us  [the longest x1 7.09 us: body(): lax.all_to_all(by_row, 'col', 0, 0, tiled=True)]
    scatter-add x2 -> x0, other arithmetic: 10.4 us -> none  [spread_blocks(): return empty.at[rows_at[:, None], cols_at[None, :]].add(values)]
  transfers between devices with their start and end apart: 6 -> 14, of which waited for: 4 -> 8; matrix products, arithmetic and copies ran while one was open for 8% -> 3% of each run, Pallas kernels for 0% -> 9%
where the time goes in v1:
time: 133 us; the launch traced here: 132 us
  waiting for transfers between devices  59.3 us (45%)
  starting transfers between devices  50 us (38%)
  Pallas kernels  15.9 us (12%)
  local copies, waits for them, and re-layouts  5.48 us (4%)
    all_to_all x1, waiting for transfers between devices, body(): lax.all_to_all(by_row, 'col', 0, 0, tiled=True)  28.2 us
    ppermute x8, starting transfers between devices, shift(): lax.ppermute(value, axis, [(i, (i + by) % size) for i in range(size)])  27.2 us
    ppermute x4, starting transfers between devices, body(): to_sibling = lambda v: lax.ppermute(v, 'leaf', pairs)  11.4 us
    ppermute x4, waiting for transfers between devices, body(): to_sibling = lambda v: lax.ppermute(v, 'leaf', pairs)  11 us
    ppermute x8, waiting for transfers between devices, shift(): lax.ppermute(value, axis, [(i, (i + by) % size) for i in range(size)])  10.2 us
    all_to_all x1, waiting for transfers between devices, body(): by_row = lax.all_to_all(masked, 'row', 0, 0, tiled=True)  9.84 us
    pallas_call x4, Pallas kernels, update(): pl.pallas_call(functools.partial(update_kernel, counts, firsts), out_shap...  7.26 us
    all_to_all x1, starting transfers between devices, body(): lax.all_to_all(by_row, 'col', 0, 0, tiled=True)  7.09 us
  transfers between devices with their start and end apart: 14, of which 8 were waited for; matrix products, arithmetic and copies ran while one was open for 3% of the time, Pallas kernels for 9%

profile of v1, /device:TPU:448, one launch (start us, length us, event | category | flops | bytes accessed | tf_op | source)
XLA Modules:
  0.0 131.7 jit_solution(7455627529660145741)
XLA Ops:
  0.0 0.0 copy-start.1
  0.0 1.2 copy-done.1
  1.2 0.0 copy-start.2
  1.2 0.7 copy-done.2
  1.9 1.8 %shard_map.55 = (f32[1024,256]{1,0:T(8,128)}, f32[512,256]{1,0:T(8,128)}) custom-call(s32[2,8]{1,0:T(2,128)S(1)} %bitcast.26, f32[1024,256]{1,0:T(8,128)S(1)} %copy-done.1), custom_call_target="tpu_custom_call" | custom-call | flops 1500000000 | bytes 3000000 | tf_op jit(solution)/shard_map/pallas_call | solution.py:41
  3.7 0.0 copy-start.4
  3.7 4.4 %all-to-all-start = ((f32[4,256,256]{2,1,0:T(8,128)}), f32[4,256,256]{2,1,0:T(8,128)}, u32[]{:S(2)}, u32[]{:S(2)}) async-start(f32[4,256,256]{2,1,0:T(8,128)} %bitcast.12), calls=%async_computation | async-start | bytes 2097152 | tf_op jit(solution)/shard_map/all_to_all | solution.py:188
  8.1 0.0 copy-done.4
  8.1 0.0 copy-start.3
  8.1 3.6 %collective-permute-start = (s32[1,12]{1,0:T(1,128)S(1)}, s32[1,12]{1,0:T(1,128)S(1)}, u32[]{:S(2)}, u32[]{:S(2)}) collective-permute-start(s32[1,12]{1,0:T(1,128)S(1)} %copy-done.4), channel_id=1, source_target_pairs={{0,256},{16,272},{32,288},{48,304},{64,320},{80,336},{96,352},{112... | collective-permute-start | bytes 152 | tf_op jit(solution)/shard_map/ppermute | solution.py:184
  11.7 1.9 %collective-permute-done = s32[1,12]{1,0:T(1,128)S(1)} collective-permute-done((s32[1,12]{1,0:T(1,128)S(1)}, s32[1,12]{1,0:T(1,128)S(1)}, u32[]{:S(2)}, u32[]{:S(2)}) %collective-permute-start) | collective-permute-done | bytes 80 | tf_op jit(solution)/shard_map/ppermute | solution.py:184
  13.7 9.8 %all-to-all-done = f32[4,256,256]{2,1,0:T(8,128)} async-done(((f32[4,256,256]{2,1,0:T(8,128)}), f32[4,256,256]{2,1,0:T(8,128)}, u32[]{:S(2)}, u32[]{:S(2)}) %all-to-all-start) | async-done | bytes 1048608 | tf_op jit(solution)/shard_map/all_to_all | solution.py:188
  23.5 7.1 %all-to-all-start.1 = ((f32[4,256,256]{2,1,0:T(8,128)}), f32[4,256,256]{2,1,0:T(8,128)S(1)}, u32[]{:S(2)}, u32[]{:S(2)}) async-start(f32[4,256,256]{2,1,0:T(8,128)} %bitcast.14), calls=%async_computation.1 | async-start | bytes 2097152 | tf_op jit(solution)/shard_map/all_to_all | solution.py:190
  30.6 6.0 %collective-permute-start.2 = (f32[512,256]{1,0:T(8,128)}, f32[512,256]{1,0:T(8,128)}, u32[]{:S(2)}, u32[]{:S(2)}) collective-permute-start(f32[512,256]{1,0:T(8,128)} %get-tuple-element.17.refs_0_), channel_id=1, source_target_pairs={{0,3},{1,0},{2,1},{3,2},{4,7},{5,4},{6,5},{7,6},{8,11},{9,8},{10,9... | collective-permute-start | bytes 1572872 | tf_op jit(solution)/shard_map/ppermute | solution.py:26
  36.6 1.9 %collective-permute-start.1 = (f32[512,256]{1,0:T(8,128)}, f32[512,256]{1,0:T(8,128)}, u32[]{:S(2)}, u32[]{:S(2)}) collective-permute-start(f32[512,256]{1,0:T(8,128)} %get-tuple-element.17.refs_0_), channel_id=1, source_target_pairs={{0,1},{1,2},{2,3},{3,0},{4,5},{5,6},{6,7},{7,4},{8,9},{9,10},{10,1... | collective-permute-start | bytes 1572872 | tf_op jit(solution)/shard_map/ppermute | solution.py:26
  38.6 0.0 copy-done.3
  38.6 28.2 %all-to-all-done.1.refs_0_ = f32[4,256,256]{2,1,0:T(8,128)S(1)} async-done(((f32[4,256,256]{2,1,0:T(8,128)}), f32[4,256,256]{2,1,0:T(8,128)S(1)}, u32[]{:S(2)}, u32[]{:S(2)}) %all-to-all-start.1) | async-done | bytes 1048608 | tf_op jit(solution)/shard_map/all_to_all | solution.py:190
  66.8 3.1 %collective-permute-start.4 = (f32[4,256,256]{2,1,0:T(8,128)S(1)}, f32[4,256,256]{2,1,0:T(8,128)S(1)}, u32[]{:S(2)}, u32[]{:S(2)}) collective-permute-start(f32[4,256,256]{2,1,0:T(8,128)S(1)} %all-to-all-done.1.refs_0_), channel_id=1, source_target_pairs={{0,12},{4,0},{8,4},{12,8},{1,13},{5,1},{9,5},{13,9},{2,14},{6,2},{... | collective-permute-start | bytes 3145736 | tf_op jit(solution)/shard_map/ppermute | solution.py:26
  69.9 2.8 %collective-permute-start.3 = (f32[4,256,256]{2,1,0:T(8,128)S(1)}, f32[4,256,256]{2,1,0:T(8,128)S(1)}, u32[]{:S(2)}, u32[]{:S(2)}) collective-permute-start(f32[4,256,256]{2,1,0:T(8,128)S(1)} %all-to-all-done.1.refs_0_), channel_id=1, source_target_pairs={{0,4},{4,8},{8,12},{12,0},{1,5},{5,9},{9,13},{13,1},{2,6},{6,10},{... | collective-permute-start | bytes 3145736 | tf_op jit(solution)/shard_map/ppermute | solution.py:26
  72.7 0.1 pad_add_fusion.1.quarter_ref
  72.8 0.1 add_multiply_fusion
  72.9 0.1 iota_add_fusion
  73.0 5.2 %collective-permute-done.2.refs_2_ = f32[512,256]{1,0:T(8,128)} collective-permute-done((f32[512,256]{1,0:T(8,128)}, f32[512,256]{1,0:T(8,128)}, u32[]{:S(2)}, u32[]{:S(2)}) %collective-permute-start.2) | collective-permute-done | bytes 524320 | tf_op jit(solution)/shard_map/ppermute | solution.py:26
  78.2 1.7 %slice.31 = f32[256,256]{1,0:T(8,128)} slice(f32[512,256]{1,0:T(8,128)} %collective-permute-done.2.refs_2_), slice={[256:512], [0:256]} | slice | bytes 524288 | tf_op jit(solution)/shard_map/slice | solution.py:193
  79.8 3.3 %collective-permute-start.6 = (f32[256,256]{1,0:T(8,128)}, f32[256,256]{1,0:T(8,128)S(1)}, u32[]{:S(2)}, u32[]{:S(2)}) collective-permute-start(f32[256,256]{1,0:T(8,128)} %slice.31), channel_id=1, source_target_pairs={{0,3},{1,0},{2,1},{3,2},{4,7},{5,4},{6,5},{7,6},{8,11},{9,8},{10,9... | collective-permute-start | bytes 786440 | tf_op jit(solution)/shard_map/ppermute | solution.py:26
  83.2 0.0 collective-permute-done.1.refs_1_
  83.2 1.7 %slice.30 = f32[256,256]{1,0:T(8,128)} slice(f32[512,256]{1,0:T(8,128)} %collective-permute-done.1.refs_1_), slice={[0:256], [0:256]} | slice | bytes 524288 | tf_op jit(solution)/shard_map/slice | solution.py:193
  84.9 3.8 %collective-permute-start.5 = (f32[256,256]{1,0:T(8,128)}, f32[256,256]{1,0:T(8,128)}, u32[]{:S(2)}, u32[]{:S(2)}) collective-permute-start(f32[256,256]{1,0:T(8,128)} %slice.30), channel_id=1, source_target_pairs={{0,1},{1,2},{2,3},{3,0},{4,5},{5,6},{6,7},{7,4},{8,9},{9,10},{10,1... | collective-permute-start | bytes 786440 | tf_op jit(solution)/shard_map/ppermute | solution.py:26
  88.7 0.1 pad_add_fusion.place_ref
  88.8 0.1 add.90
  88.8 0.1 select_reduce_fusion.2.from_ref
  89.0 1.6 %shard_map.56 = (bf16[3,512,256]{2,1,0:T(8,128)(2,1)S(1)}, bf16[3,512,256]{2,1,0:T(8,128)(2,1)S(1)}) custom-call(s32[4]{0:T(128)S(1)} %compare_select_fusion.to_ref, f32[512,256]{1,0:T(8,128)} %get-tuple-element.17.refs_0_, f32[512,256]{1,0:T(8,128)} %collective-permute-done.1.refs_1_, f32[512,256]{1,0:T(8,128)} %collective-permute-done.2.refs_2_), custom_call_target="tpu_custom_call" | custom-call | flops 1200000000 | bytes 2400000 | tf_op jit(solution)/shard_map/pallas_call | solution.py:75
  90.5 0.0 copy-start
  90.5 3.0 %collective-permute-done.4.refs_1_ = f32[4,256,256]{2,1,0:T(8,128)S(1)} collective-permute-done((f32[4,256,256]{2,1,0:T(8,128)S(1)}, f32[4,256,256]{2,1,0:T(8,128)S(1)}, u32[]{:S(2)}, u32[]{:S(2)}) %collective-permute-start.4) | collective-permute-done | bytes 1048608 | tf_op jit(solution)/shard_map/ppermute | solution.py:26
  93.6 4.3 %collective-permute-start.8 = (f32[2,256,256]{2,1,0:T(8,128)S(1)}, f32[2,256,256]{2,1,0:T(8,128)S(1)}, u32[]{:S(2)}, u32[]{:S(2)}) collective-permute-start(f32[2,256,256]{2,1,0:T(8,128)S(1)} %slice.33), channel_id=1, source_target_pairs={{0,12},{4,0},{8,4},{12,8},{1,13},{5,1},{9,5},{13,9},{2,14},{6,2},{... | collective-permute-start | bytes 1572872 | tf_op jit(solution)/shard_map/ppermute | solution.py:26
  97.9 0.0 collective-permute-done.3.refs_0_
  97.9 1.9 %collective-permute-start.7 = (f32[2,256,256]{2,1,0:T(8,128)S(1)}, f32[2,256,256]{2,1,0:T(8,128)S(1)}, u32[]{:S(2)}, u32[]{:S(2)}) collective-permute-start(f32[2,256,256]{2,1,0:T(8,128)S(1)} %slice.32), channel_id=1, source_target_pairs={{0,4},{4,8},{8,12},{12,0},{1,5},{5,9},{9,13},{13,1},{2,6},{6,10},{... | collective-permute-start | bytes 1572872 | tf_op jit(solution)/shard_map/ppermute | solution.py:26
  99.9 0.0 collective-permute-done.6.refs_1_
  99.9 0.0 collective-permute-done.5.refs_0_
  99.9 1.0 shard_map.57
  100.9 0.0 copy-done
  100.9 2.8 %shard_map.60 = (f32[256,512]{1,0:T(8,128)S(1)}, f32[256,512]{1,0:T(8,128)S(1)}) custom-call(s32[2]{0:T(128)S(1)} %pad_add_fusion.1.quarter_ref, s32[4]{0:T(128)S(1)} %select_reduce_fusion.2.from_ref, s32[4]{0:T(128)S(1)} %pad_add_fusion.place_ref, bf16[3,512,256]{2,1,0:T(8,128)(2,1)S(1)} %get-tuple-element.18.near_high, ...), custom_call_target="tpu_custom_call" | custom-call | flops 3200000000 | bytes 6400000 | tf_op jit(solution)/shard_map/pallas_call | solution.py:121
  103.7 2.2 %collective-permute-start.11 = (f32[256,512]{1,0:T(8,128)S(1)}, f32[256,512]{1,0:T(8,128)S(1)}, u32[]{:S(2)}, u32[]{:S(2)}) collective-permute-start(f32[256,512]{1,0:T(8,128)S(1)} %get-tuple-element.28), channel_id=1, source_target_pairs={{0,256},{16,272},{32,288},{48,304},{64,320},{80,336},{96,352},{112... | collective-permute-start | bytes 1572872 | tf_op jit(solution)/shard_map/ppermute | solution.py:184
  106.0 1.7 %shard_map.59 = (f32[256,256]{1,0:T(8,128)S(1)}, f32[256,256]{1,0:T(8,128)S(1)}) custom-call(s32[1]{0:T(128)} %bitcast.quarter_ref, s32[4]{0:T(128)S(1)} %select_reduce_fusion.2.from_ref, s32[4]{0:T(128)S(1)} %pad_add_fusion.place_ref, bf16[3,512,256]{2,1,0:T(8,128)(2,1)S(1)} %get-tuple-element.18.near_high, ...), custom_call_target="tpu_custom_call" | custom-call | flops 1600000000 | bytes 3200000 | tf_op jit(solution)/shard_map/pallas_call | solution.py:121
  107.7 3.6 %collective-permute-start.10 = (f32[256,256]{1,0:T(8,128)S(1)}, f32[256,256]{1,0:T(8,128)S(1)}, u32[]{:S(2)}, u32[]{:S(2)}) collective-permute-start(f32[256,256]{1,0:T(8,128)S(1)} %get-tuple-element.27), channel_id=1, source_target_pairs={{0,256},{16,272},{32,288},{48,304},{64,320},{80,336},{96,352},{112... | collective-permute-start | bytes 786440 | tf_op jit(solution)/shard_map/ppermute | solution.py:184
  111.4 0.2 select_reduce_fusion
  111.5 0.1 slice.24.slots_ref
  111.6 0.0 collective-permute-done.8.refs_1_
  111.6 2.0 %collective-permute-done.7.refs_0_ = f32[2,256,256]{2,1,0:T(8,128)S(1)} collective-permute-done((f32[2,256,256]{2,1,0:T(8,128)S(1)}, f32[2,256,256]{2,1,0:T(8,128)S(1)}, u32[]{:S(2)}, u32[]{:S(2)}) %collective-permute-start.7) | collective-permute-done | bytes 524320 | tf_op jit(solution)/shard_map/ppermute | solution.py:26
  113.6 1.4 %shard_map.58 = f32[256,256]{1,0:T(8,128)S(1)} custom-call(s32[1]{0:T(128)} %bitcast.3.quarter_ref, s32[4]{0:T(128)S(1)} %select_reduce_fusion.2.from_ref, s32[4]{0:T(128)S(1)} %pad_add_fusion.place_ref, bf16[3,512,256]{2,1,0:T(8,128)(2,1)S(1)} %get-tuple-element.18.near_high, bf16[3,512,256]{2,1,0:T(8,128)(2,1)S(1)} %get-tuple-element.19.near_low, ...), custom_call_target="tpu_custom_call" | custom-call | flops 1000000000 | bytes 2000000 | tf_op jit(solution)/shard_map/pallas_call | solution.py:121
  115.0 1.9 %collective-permute-start.9 = (f32[256,256]{1,0:T(8,128)S(1)}, f32[256,256]{1,0:T(8,128)S(1)}, u32[]{:S(2)}, u32[]{:S(2)}) collective-permute-start(f32[256,256]{1,0:T(8,128)S(1)} %shard_map.58), channel_id=1, source_target_pairs={{0,256},{16,272},{32,288},{48,304},{64,320},{80,336},{96,352},{112... | collective-permute-start | bytes 786440 | tf_op jit(solution)/shard_map/ppermute | solution.py:184
  116.9 1.4 %shard_map.61.refs_2_ = f32[256,256]{1,0:T(8,128)S(1)} custom-call(s32[1]{0:T(128)} %bitcast.3.quarter_ref, s32[4]{0:T(128)S(1)} %select_reduce_fusion.2.from_ref, s32[4]{0:T(128)S(1)} %pad_add_fusion.place_ref, bf16[3,512,256]{2,1,0:T(8,128)(2,1)S(1)} %get-tuple-element.18.near_high, bf16[3,512,256]{2,1,0:T(8,128)(2,1)S(1)} %get-tuple-element.19.near_low, ...), custom_call_target="tpu_custom_call" | custom-call | flops 1000000000 | bytes 2000000 | tf_op jit(solution)/shard_map/pallas_call | solution.py:121
  118.3 7.8 %collective-permute-done.10.refs_3_ = f32[256,256]{1,0:T(8,128)S(1)} collective-permute-done((f32[256,256]{1,0:T(8,128)S(1)}, f32[256,256]{1,0:T(8,128)S(1)}, u32[]{:S(2)}, u32[]{:S(2)}) %collective-permute-start.10) | collective-permute-done | bytes 262176 | tf_op jit(solution)/shard_map/ppermute | solution.py:184
  126.1 0.0 collective-permute-done.11.refs_4_
  126.1 2.1 %shard_map.62.sum_ref = f32[256,1536]{1,0:T(8,128)} custom-call(s32[8]{0:T(128)S(1)} %get-tuple-element.29.mine_ref, s32[8]{0:T(128)S(1)} %get-tuple-element.30.other_ref, f32[256,256]{1,0:T(8,128)S(1)} %get-tuple-element.25.refs_0_, f32[256,512]{1,0:T(8,128)S(1)} %get-tuple-element.26.refs_1_, f32[256,256]{1,0:T(8,128)S(1)} %shard_map.61.refs_2_, ...), custom_call_target="tpu_custom_call" | custom-call | flops 2000000000 | bytes 4000000 | tf_op jit(solution)/shard_map/pallas_call | solution.py:145
  128.2 1.3 collective-permute-done.9.value_ref
  129.4 2.2 %shard_map.63 = f32[256,1536]{1,0:T(8,128)} custom-call(s32[2]{0:T(128)S(1)} %slice.24.slots_ref, f32[256,256]{1,0:T(8,128)S(1)} %collective-permute-done.9.value_ref, f32[256,1536]{1,0:T(8,128)} %shard_map.62.sum_ref), custom_call_target="tpu_custom_call", output_to_operand_aliasing={{}: (2, {})} | custom-call | flops 1000000000 | bytes 2000000 | tf_op jit(solution)/shard_map/pallas_call | solution.py:162
  (6 shorter events, 0.1 us)
Async XLA Ops:
  0.0 1.2 copy-start.1
  1.2 0.7 copy-start.2
  3.7 4.4 %copy-start.4 = (s32[1,12]{1,0:T(1,128)S(1)}, s32[1,12]{1,0:T(1,128)}, u32[]{:S(2)}) copy-start(s32[1,12]{1,0:T(1,128)} %param.9) | copy-start | bytes 148
  3.7 19.8 %all-to-all-start = ((f32[4,256,256]{2,1,0:T(8,128)}), f32[4,256,256]{2,1,0:T(8,128)}, u32[]{:S(2)}, u32[]{:S(2)}) async-start(f32[4,256,256]{2,1,0:T(8,128)} %bitcast.12), calls=%async_computation | async-start | bytes 2097152 | tf_op jit(solution)/shard_map/all_to_all | solution.py:188
  8.1 30.5 %copy-start.3 = (s32[1,4]{1,0:T(1,128)S(1)}, s32[1,4]{1,0:T(1,128)}, u32[]{:S(2)}) copy-start(s32[1,4]{1,0:T(1,128)} %param.8) | copy-start | bytes 52
  8.1 5.6 %collective-permute-start = (s32[1,12]{1,0:T(1,128)S(1)}, s32[1,12]{1,0:T(1,128)S(1)}, u32[]{:S(2)}, u32[]{:S(2)}) collective-permute-start(s32[1,12]{1,0:T(1,128)S(1)} %copy-done.4), channel_id=1, source_target_pairs={{0,256},{16,272},{32,288},{48,304},{64,320},{80,336},{96,352},{112... | collective-permute-start | bytes 152 | tf_op jit(solution)/shard_map/ppermute | solution.py:184
  23.5 43.3 %all-to-all-start.1 = ((f32[4,256,256]{2,1,0:T(8,128)}), f32[4,256,256]{2,1,0:T(8,128)S(1)}, u32[]{:S(2)}, u32[]{:S(2)}) async-start(f32[4,256,256]{2,1,0:T(8,128)} %bitcast.14), calls=%async_computation.1 | async-start | bytes 2097152 | tf_op jit(solution)/shard_map/all_to_all | solution.py:190
  30.6 47.6 %collective-permute-start.2 = (f32[512,256]{1,0:T(8,128)}, f32[512,256]{1,0:T(8,128)}, u32[]{:S(2)}, u32[]{:S(2)}) collective-permute-start(f32[512,256]{1,0:T(8,128)} %get-tuple-element.17.refs_0_), channel_id=1, source_target_pairs={{0,3},{1,0},{2,1},{3,2},{4,7},{5,4},{6,5},{7,6},{8,11},{9,8},{10,9... | collective-permute-start | bytes 1572872 | tf_op jit(solution)/shard_map/ppermute | solution.py:26
  36.6 46.5 %collective-permute-start.1 = (f32[512,256]{1,0:T(8,128)}, f32[512,256]{1,0:T(8,128)}, u32[]{:S(2)}, u32[]{:S(2)}) collective-permute-start(f32[512,256]{1,0:T(8,128)} %get-tuple-element.17.refs_0_), channel_id=1, source_target_pairs={{0,1},{1,2},{2,3},{3,0},{4,5},{5,6},{6,7},{7,4},{8,9},{9,10},{10,1... | collective-permute-start | bytes 1572872 | tf_op jit(solution)/shard_map/ppermute | solution.py:26
  66.8 26.7 %collective-permute-start.4 = (f32[4,256,256]{2,1,0:T(8,128)S(1)}, f32[4,256,256]{2,1,0:T(8,128)S(1)}, u32[]{:S(2)}, u32[]{:S(2)}) collective-permute-start(f32[4,256,256]{2,1,0:T(8,128)S(1)} %all-to-all-done.1.refs_0_), channel_id=1, source_target_pairs={{0,12},{4,0},{8,4},{12,8},{1,13},{5,1},{9,5},{13,9},{2,14},{6,2},{... | collective-permute-start | bytes 3145736 | tf_op jit(solution)/shard_map/ppermute | solution.py:26
  69.9 28.0 %collective-permute-start.3 = (f32[4,256,256]{2,1,0:T(8,128)S(1)}, f32[4,256,256]{2,1,0:T(8,128)S(1)}, u32[]{:S(2)}, u32[]{:S(2)}) collective-permute-start(f32[4,256,256]{2,1,0:T(8,128)S(1)} %all-to-all-done.1.refs_0_), channel_id=1, source_target_pairs={{0,4},{4,8},{8,12},{12,0},{1,5},{5,9},{9,13},{13,1},{2,6},{6,10},{... | collective-permute-start | bytes 3145736 | tf_op jit(solution)/shard_map/ppermute | solution.py:26
  79.8 20.1 %collective-permute-start.6 = (f32[256,256]{1,0:T(8,128)}, f32[256,256]{1,0:T(8,128)S(1)}, u32[]{:S(2)}, u32[]{:S(2)}) collective-permute-start(f32[256,256]{1,0:T(8,128)} %slice.31), channel_id=1, source_target_pairs={{0,3},{1,0},{2,1},{3,2},{4,7},{5,4},{6,5},{7,6},{8,11},{9,8},{10,9... | collective-permute-start | bytes 786440 | tf_op jit(solution)/shard_map/ppermute | solution.py:26
  84.9 15.0 %collective-permute-start.5 = (f32[256,256]{1,0:T(8,128)}, f32[256,256]{1,0:T(8,128)}, u32[]{:S(2)}, u32[]{:S(2)}) collective-permute-start(f32[256,256]{1,0:T(8,128)} %slice.30), channel_id=1, source_target_pairs={{0,1},{1,2},{2,3},{3,0},{4,5},{5,6},{6,7},{7,4},{8,9},{9,10},{10,1... | collective-permute-start | bytes 786440 | tf_op jit(solution)/shard_map/ppermute | solution.py:26
  90.5 10.4 %copy-start = (f32[512,1024]{1,0:T(8,128)S(1)}, f32[512,1024]{1,0:T(8,128)}, u32[]{:S(2)}) copy-start(f32[512,1024]{1,0:T(8,128)} %front_ref.7) | copy-start | bytes 6291460
  93.6 18.0 %collective-permute-start.8 = (f32[2,256,256]{2,1,0:T(8,128)S(1)}, f32[2,256,256]{2,1,0:T(8,128)S(1)}, u32[]{:S(2)}, u32[]{:S(2)}) collective-permute-start(f32[2,256,256]{2,1,0:T(8,128)S(1)} %slice.33), channel_id=1, source_target_pairs={{0,12},{4,0},{8,4},{12,8},{1,13},{5,1},{9,5},{13,9},{2,14},{6,2},{... | collective-permute-start | bytes 1572872 | tf_op jit(solution)/shard_map/ppermute | solution.py:26
  97.9 15.7 %collective-permute-start.7 = (f32[2,256,256]{2,1,0:T(8,128)S(1)}, f32[2,256,256]{2,1,0:T(8,128)S(1)}, u32[]{:S(2)}, u32[]{:S(2)}) collective-permute-start(f32[2,256,256]{2,1,0:T(8,128)S(1)} %slice.32), channel_id=1, source_target_pairs={{0,4},{4,8},{8,12},{12,0},{1,5},{5,9},{9,13},{13,1},{2,6},{6,10},{... | collective-permute-start | bytes 1572872 | tf_op jit(solution)/shard_map/ppermute | solution.py:26
  103.7 22.4 %collective-permute-start.11 = (f32[256,512]{1,0:T(8,128)S(1)}, f32[256,512]{1,0:T(8,128)S(1)}, u32[]{:S(2)}, u32[]{:S(2)}) collective-permute-start(f32[256,512]{1,0:T(8,128)S(1)} %get-tuple-element.28), channel_id=1, source_target_pairs={{0,256},{16,272},{32,288},{48,304},{64,320},{80,336},{96,352},{112... | collective-permute-start | bytes 1572872 | tf_op jit(solution)/shard_map/ppermute | solution.py:184
  107.7 18.4 %collective-permute-start.10 = (f32[256,256]{1,0:T(8,128)S(1)}, f32[256,256]{1,0:T(8,128)S(1)}, u32[]{:S(2)}, u32[]{:S(2)}) collective-permute-start(f32[256,256]{1,0:T(8,128)S(1)} %get-tuple-element.27), channel_id=1, source_target_pairs={{0,256},{16,272},{32,288},{48,304},{64,320},{80,336},{96,352},{112... | collective-permute-start | bytes 786440 | tf_op jit(solution)/shard_map/ppermute | solution.py:184
  115.0 14.5 %collective-permute-start.9 = (f32[256,256]{1,0:T(8,128)S(1)}, f32[256,256]{1,0:T(8,128)S(1)}, u32[]{:S(2)}, u32[]{:S(2)}) collective-permute-start(f32[256,256]{1,0:T(8,128)S(1)} %shard_map.58), channel_id=1, source_target_pairs={{0,256},{16,272},{32,288},{48,304},{64,320},{80,336},{96,352},{112... | collective-permute-start | bytes 786440 | tf_op jit(solution)/shard_map/ppermute | solution.py:184

commit v2 on v1

--- a/solution.py
+++ b/solution.py
@@ -57,35 +57,46 @@
     return high, (value - high.astype(F32)).astype(BF16)
 
 
-def window_kernel(groups, to_ref, *refs):
-    pieces, (high_ref, low_ref) = refs[:-2], refs[-2:]
+def window_kernel(groups, count, to_ref, *refs):
+    pieces, (high_ref, low_ref), extra = refs[:count], refs[count : count + 2], refs[count + 2 :]
     for d in range(groups):
-        per = len(pieces) // groups
+        per = count // groups
         j = 0
         for piece in pieces[d * per : (d + 1) * per]:
             for i in range(piece.shape[0] // BLK):
                 at = pl.ds(pl.multiple_of(to_ref[j] * BLK, BLK), BLK)
                 high_ref[d, at], low_ref[d, at] = halves(piece[pl.ds(i * BLK, BLK)])
                 j += 1
-
-
-def split_window(to, groups, *pieces):
-    rows = sum(p.shape[0] for p in pieces) // groups
-    out = jax.ShapeDtypeStruct((groups, rows, pieces[0].shape[1]), BF16)
-    return pl.pallas_call(
-        functools.partial(window_kernel, groups),
-        out_shape=[out, out],
+    if extra:
+        first_ref, second_ref = extra
+        rows = first_ref.shape[0]
+        first_ref[...] = pieces[1][pl.ds(0, rows)]
+        second_ref[...] = pieces[2][pl.ds(rows, rows)]
+
+
+def split_window(to, groups, us, *pieces, forward=False):
+    rows, width = sum(p.shape[0] for p in pieces) // groups, pieces[0].shape[1]
+    out = [jax.ShapeDtypeStruct((groups, rows, width), BF16)] * 2
+    if forward:
+        out += [jax.ShapeDtypeStruct((rows // 2, width), F32)] * 2
+    return pl.pallas_call(
+        functools.partial(window_kernel, groups, len(pieces)),
+        out_shape=out,
         in_specs=[SMEM] + [VMEM] * len(pieces),
-        out_specs=[VMEM, VMEM],
-        compiler_params=pltpu.CompilerParams(vmem_limit_bytes=LIMIT),
-        cost_estimate=cost(0.4 * groups),
+        out_specs=[VMEM] * len(out),
+        compiler_params=pltpu.CompilerParams(vmem_limit_bytes=LIMIT),
+        cost_estimate=cost(us),
     )(to, *pieces)
 
 
-def update_kernel(counts, firsts, quarter_ref, from_ref, place_ref, near_high, near_low, far_high, far_low, front_ref, *refs):
+def update_kernel(counts, firsts, extra, quarter_ref, from_ref, place_ref, near_high, near_low, far_high, far_low, front_ref, *refs):
     (big_ref, small_ref), refs = refs[-2:], refs[:-2]
+    if extra:
+        extra_ref, refs = refs[0], refs[1:]
     pieces, outs = refs[: sum(map(len, counts))], refs[sum(map(len, counts)) :]
-    rows, width = outs[0].shape[0], outs[0].shape[1] // len(counts)
+    rows, width = front_ref.shape[0] // 2, outs[0].shape[1] // len(counts)
+    if extra:
+        outs[0][pl.ds(rows, extra)] = extra_ref[...]
     first, span = firsts[0] * BLK, rows * len(outs)
     near = near_high.shape[0]
     for q, parts in enumerate(counts):
@@ -114,19 +125,20 @@
                 )
 
 
-def update(quarters, sources, place, window, front, groups, firsts, us):
+def update(quarters, sources, place, window, front, groups, firsts, us, *extra):
     counts = tuple(tuple(p.shape[0] for p in group) for group in groups)
     pieces = [p for group in groups for p in group]
-    out = jax.ShapeDtypeStruct((front.shape[0] // 2, len(groups) * pieces[0].shape[1]), F32)
-    return pl.pallas_call(
-        functools.partial(update_kernel, counts, firsts),
+    more = sum(e.shape[0] for e in extra)
+    out = jax.ShapeDtypeStruct((front.shape[0] // 2 + more, len(groups) * pieces[0].shape[1]), F32)
+    return pl.pallas_call(
+        functools.partial(update_kernel, counts, firsts, more),
         out_shape=[out] * len(firsts),
-        in_specs=[SMEM] * 3 + [VMEM] * (5 + len(pieces)),
+        in_specs=[SMEM] * 3 + [VMEM] * (5 + len(extra) + len(pieces)),
         out_specs=[VMEM] * len(firsts),
         scratch_shapes=[pltpu.VMEM((len(groups), sum(counts[0]), *pieces[0].shape[1:]), BF16)] * 2,
         compiler_params=pltpu.CompilerParams(vmem_limit_bytes=LIMIT),
         cost_estimate=cost(us),
-    )(quarters, sources, place, *window, front, *pieces)
+    )(quarters, sources, place, *window, front, *extra, *pieces)
 
 
 def place_kernel(count, mine_ref, other_ref, *refs):
@@ -137,7 +149,7 @@
         start = sum(v.shape[1] for v in values[:i]) if i < count else sum(v.shape[1] for v in values[count:i])
         for j in range(value_ref.shape[1] // BLK):
             at = pl.ds(pl.multiple_of(maps_ref[start // BLK + j] * BLK, BLK), BLK)
-            value = value_ref[:, j * BLK : (j + 1) * BLK]
+            value = value_ref[pl.ds(0, out_ref.shape[0]), j * BLK : (j + 1) * BLK]
             out_ref[:, at] = value if i < count else out_ref[:, at] + value
 
 
@@ -184,40 +196,44 @@
     to_sibling = lambda v: lax.ppermute(v, "leaf", pairs)
 
     masked, window = mask_rows(block_mask, panel, win_rows)
-    other_maps = to_sibling(col_maps)
     by_row = lax.all_to_all(masked, "row", 0, 0, tiled=True)
-    by_row = after_all(by_row, other_maps)
     mine = lax.all_to_all(by_row, "col", 0, 0, tiled=True).reshape(n_col, columns, width)
-    half = win_rows // 2
     before, after = shift(window, "col", 1), shift(window, "col", -1)
-    far_low, far_high = shift(before[:half], "col", 1), shift(after[half:], "col", -1)
-    q_before, q_after = shift(mine, "row", 1), shift(mine, "row", -1)
-    q_low, q_high = shift(q_before[: n_col // 2], "row", 1), shift(q_after[n_col // 2 :], "row", -1)
-
     target = row_maps[0]
     to = jnp.where(target // 2 == upper, target % 2, 2 + target % 2).astype(jnp.int32)
     sources = jnp.sum(
         jnp.where(to[None, :] == jnp.arange(to.shape[0])[:, None], jnp.arange(to.shape[0])[None, :], 0), 1
     ).astype(jnp.int32)
+    *near, low, high = split_window(to, 3, 60, window, before, after, forward=True)
+    mine = after_all(mine, low)
+    far_low, far_high = shift(low, "col", 1), shift(high, "col", -1)
+    lower, upper_half = mine[: n_col // 2], mine[n_col // 2 :]
+    b_low, a_high = shift(lower, "row", 1), shift(upper_half, "row", -1)
+    b_high, a_low = shift(upper_half, "row", 1), shift(lower, "row", -1)
+    q_low, q_high = shift(b_low, "row", 1), shift(a_high, "row", -1)
+
     place = jnp.stack([col, (col + n_col - 1) % n_col, (col + 1) % n_col, (col + 2) % n_col]).astype(jnp.int32)
-    window = (*split_window(to, 3, window, before, after), *split_window(after_all(to, q_before, q_after), 1, far_low, far_high))
+    window = (*near, *split_window(after_all(to, b_low, a_high), 1, 0.5, far_low, far_high))
 
     quarters = jnp.stack([row, (row + n_row - 1) % n_row, (row + 1) % n_row, (row + 2) % n_row]).astype(jnp.int32)
     half = win_rows // BLK // 2
-    keep0, send0 = update(quarters[:1], sources, place, window, front_rest, ((mine,),), (0, half), 1.6)
+    maps_rows = jnp.pad(col_maps.astype(F32), ((0, 7), (0, columns - col_maps.shape[1])))
+    (send0,) = update(quarters[:1], sources, place, window, front_rest, ((mine,),), (half,), 1, maps_rows)
     got0 = to_sibling(send0)
-    keep1, send1 = update(quarters[1:3], sources, place, window, front_rest, ((q_before,), (q_after,)), (0, half), 3.2)
+    pair, last = ((b_low, b_high), (a_low, a_high)), ((q_low, q_high),)
+    (send1,) = update(after_all(quarters[1:3], send0), sources, place, window, front_rest, pair, (half,), 2)
     got1 = to_sibling(send1)
-    last = ((q_low, q_high),)
     (send2,) = update(quarters[3:], sources, place, window, front_rest, last, (half,), 1)
     got2 = to_sibling(send2)
-    (keep2,) = update(quarters[3:], sources, place, window, front_rest, last, (0,), 1)
+    (keep,) = update(after_all(quarters, send2), sources, place, window, front_rest, ((mine,), *pair, *last), (0,), 4)
+    got0 = after_all(got0, keep)
+    other_maps = got0[-8:-7, : col_maps.shape[1]].astype(jnp.int32)
 
     per = columns // BLK
     order = (quarters[:, None] * per + jnp.arange(per)[None, :]).reshape(-1)
     pick = (order[:, None] == jnp.arange(n_row * per)[None, :]).astype(jnp.int32)
     slots, other_slots = (jnp.sum(pick * m[:, : n_row * per], 1) for m in (col_maps, other_maps))
-    total = place_blocks(slots, other_slots, (keep0, keep1, keep2), (got0, got1), PC // n_col)
+    total = place_blocks(slots, other_slots, (keep,), (got0, got1), PC // n_col)
     return add_blocks(other_slots[3 * per :], got2, total)
 
 

time: 133 us -> 127 us (0.955)
  waiting for transfers between devices: 59.3 us -> 37.2 us
  starting transfers between devices: 50 us -> 65 us
  Pallas kernels: 15.9 us -> 18.3 us
    all_to_all x1, waiting for transfers between devices: 28.2 us -> 2.69 us  [body(): lax.all_to_all(by_row, 'col', 0, 0, tiled=True)]
    ppermute x8 -> x10, starting transfers between devices: 27.2 us -> 44.6 us  [shift(): lax.ppermute(value, axis, [(i, (i + by) % size) for i in range(size)])]
    ppermute x8 -> x10, waiting for transfers between devices: 10.2 us -> 22.1 us  [shift(): lax.ppermute(value, axis, [(i, (i + by) % size) for i in range(size)])]
    ppermute x4 -> x3, waiting for transfers between devices: 11 us -> 5.26 us  [body(): to_sibling = lambda v: lax.ppermute(v, 'leaf', pairs)]
    all_to_all x1, waiting for transfers between devices: 9.84 us -> 7.07 us  [body(): by_row = lax.all_to_all(masked, 'row', 0, 0, tiled=True)]
    pallas_call x6, Pallas kernels: 9.83 us -> 12.4 us  [the longest x4 9.93 us: update(): pl.pallas_call(functools.partial(update_kernel, counts, firsts, more), ou...]
    ppermute x4 -> x3, starting transfers between devices: 11.4 us -> 8.94 us  [body(): to_sibling = lambda v: lax.ppermute(v, 'leaf', pairs)]
    slice x4 -> x1, local copies, waits for them, and re-layouts: 3.4 us -> 1.05 us  [body(): lower, upper_half = (mine[:n_col // 2], mine[n_col // 2:])]
  transfers between devices with their start and end apart: 14 -> 15, of which waited for: 8 -> 6; matrix products, arithmetic and copies ran while one was open for 3% -> 1% of each run, Pallas kernels for 9% -> 11%
where the time goes in v2:
time: 127 us; the launch traced here: 126 us
  starting transfers between devices  65 us (51%)
  waiting for transfers between devices  37.2 us (29%)
  Pallas kernels  18.3 us (14%)
  local copies, waits for them, and re-layouts  4.93 us (4%)
    ppermute x10, starting transfers between devices, shift(): lax.ppermute(value, axis, [(i, (i + by) % size) for i in range(size)])  44.6 us
    ppermute x10, waiting for transfers between devices, shift(): lax.ppermute(value, axis, [(i, (i + by) % size) for i in range(size)])  22.1 us
    pallas_call x4, Pallas kernels, update(): pl.pallas_call(functools.partial(update_kernel, counts, firsts, more), ou...  9.93 us
    ppermute x3, starting transfers between devices, body(): to_sibling = lambda v: lax.ppermute(v, 'leaf', pairs)  8.94 us
    all_to_all x1, starting transfers between devices, body(): lax.all_to_all(by_row, 'col', 0, 0, tiled=True)  7.09 us
    all_to_all x1, waiting for transfers between devices, body(): by_row = lax.all_to_all(masked, 'row', 0, 0, tiled=True)  7.07 us
    ppermute x3, waiting for transfers between devices, body(): to_sibling = lambda v: lax.ppermute(v, 'leaf', pairs)  5.26 us
    all_to_all x1, starting transfers between devices, body(): by_row = lax.all_to_all(masked, 'row', 0, 0, tiled=True)  4.42 us
  transfers between devices with their start and end apart: 15, of which 6 were waited for; matrix products, arithmetic and copies ran while one was open for 1% of the time, Pallas kernels for 11%

profile of v2, /device:TPU:448, one launch (start us, length us, event | category | flops | bytes accessed | tf_op | source)
XLA Modules:
  0.0 126.4 jit_solution(11312961110831406258)
XLA Ops:
  0.0 0.0 copy-start.5
  0.0 1.2 copy-done.5
  1.2 0.0 copy-start.6
  1.2 0.7 copy-done.6
  1.9 1.6 %shard_map.55 = (f32[1024,256]{1,0:T(8,128)}, f32[512,256]{1,0:T(8,128)S(1)}) custom-call(s32[2,8]{1,0:T(2,128)S(1)} %bitcast.24, f32[1024,256]{1,0:T(8,128)S(1)} %copy-done.5), custom_call_target="tpu_custom_call" | custom-call | flops 1500000000 | bytes 3000000 | tf_op jit(solution)/shard_map/pallas_call | solution.py:41
  3.5 0.0 copy-start.7
  3.5 4.4 %all-to-all-start = ((f32[4,256,256]{2,1,0:T(8,128)}), f32[4,256,256]{2,1,0:T(8,128)}, u32[]{:S(2)}, u32[]{:S(2)}) async-start(f32[4,256,256]{2,1,0:T(8,128)} %bitcast.11), calls=%async_computation | async-start | bytes 2097152 | tf_op jit(solution)/shard_map/all_to_all | solution.py:199
  8.0 4.5 %collective-permute-start = (f32[512,256]{1,0:T(8,128)S(1)}, f32[512,256]{1,0:T(8,128)S(1)}, u32[]{:S(2)}, u32[]{:S(2)}) collective-permute-start(f32[512,256]{1,0:T(8,128)S(1)} %get-tuple-element.18.refs_0_), channel_id=1, source_target_pairs={{0,1},{1,2},{2,3},{3,0},{4,5},{5,6},{6,7},{7,4},{8,9},{9,10},{10,1... | collective-permute-start | bytes 1572872 | tf_op jit(solution)/shard_map/ppermute | solution.py:26
  12.4 3.6 %collective-permute-start.1 = (f32[512,256]{1,0:T(8,128)S(1)}, f32[512,256]{1,0:T(8,128)S(1)}, u32[]{:S(2)}, u32[]{:S(2)}) collective-permute-start(f32[512,256]{1,0:T(8,128)S(1)} %get-tuple-element.18.refs_0_), channel_id=1, source_target_pairs={{0,3},{1,0},{2,1},{3,2},{4,7},{5,4},{6,5},{7,6},{8,11},{9,8},{10,9... | collective-permute-start | bytes 1572872 | tf_op jit(solution)/shard_map/ppermute | solution.py:26
  16.1 0.1 broadcast_multiply_fusion
  16.2 0.0 copy-done.7
  16.2 0.1 iota_add_fusion
  16.3 7.1 %all-to-all-done = f32[4,256,256]{2,1,0:T(8,128)} async-done(((f32[4,256,256]{2,1,0:T(8,128)}), f32[4,256,256]{2,1,0:T(8,128)}, u32[]{:S(2)}, u32[]{:S(2)}) %all-to-all-start) | async-done | bytes 1048608 | tf_op jit(solution)/shard_map/all_to_all | solution.py:199
  23.3 7.1 %all-to-all-start.1 = ((f32[4,256,256]{2,1,0:T(8,128)}), f32[4,256,256]{2,1,0:T(8,128)S(1)}, u32[]{:S(2)}, u32[]{:S(2)}) async-start(f32[4,256,256]{2,1,0:T(8,128)} %all-to-all-done), calls=%async_computation.1 | async-start | bytes 2097152 | tf_op jit(solution)/shard_map/all_to_all | solution.py:200
  30.4 2.8 %collective-permute-done.refs_1_ = f32[512,256]{1,0:T(8,128)S(1)} collective-permute-done((f32[512,256]{1,0:T(8,128)S(1)}, f32[512,256]{1,0:T(8,128)S(1)}, u32[]{:S(2)}, u32[]{:S(2)}) %collective-permute-start) | collective-permute-done | bytes 524320 | tf_op jit(solution)/shard_map/ppermute | solution.py:26
  33.3 19.3 %collective-permute-done.1.refs_2_ = f32[512,256]{1,0:T(8,128)S(1)} collective-permute-done((f32[512,256]{1,0:T(8,128)S(1)}, f32[512,256]{1,0:T(8,128)S(1)}, u32[]{:S(2)}, u32[]{:S(2)}) %collective-permute-start.1) | collective-permute-done | bytes 524320 | tf_op jit(solution)/shard_map/ppermute | solution.py:26
  52.6 1.4 %shard_map.56 = (bf16[3,512,256]{2,1,0:T(8,128)(2,1)S(1)}, bf16[3,512,256]{2,1,0:T(8,128)(2,1)S(1)}, f32[256,256]{1,0:T(8,128)}, f32[256,256]{1,0:T(8,128)S(1)}) custom-call(s32[4]{0:T(128)S(1)} %compare_select_fusion.to_ref, f32[512,256]{1,0:T(8,128)S(1)} %get-tuple-element.18.refs_0_, f32[512,256]{1,0:T(8,128)S(1)} %collective-permute-done.refs_1_, ...), custom_call_target="tpu_custom_call" | custom-call | flops 60000002048 | bytes 120000000 | tf_op jit(solution)/shard_map/pallas_call | solution.py:82
  54.0 0.0 copy-start.1
  54.0 0.9 copy-done.1
  54.8 0.0 copy-start.3
  54.8 0.9 copy-done.3
  55.7 0.0 copy-start.8
  55.7 0.0 copy-start
  55.7 5.5 %collective-permute-start.4 = (f32[256,256]{1,0:T(8,128)}, f32[256,256]{1,0:T(8,128)}, u32[]{:S(2)}, u32[]{:S(2)}) collective-permute-start(f32[256,256]{1,0:T(8,128)} %get-tuple-element.22), channel_id=1, source_target_pairs={{0,1},{1,2},{2,3},{3,0},{4,5},{5,6},{6,7},{7,4},{8,9},{9,10},{10,1... | collective-permute-start | bytes 786440 | tf_op jit(solution)/shard_map/ppermute | solution.py:26
  61.3 2.7 %all-to-all-done.1.refs_1_.refs_0_ = f32[4,256,256]{2,1,0:T(8,128)S(1)} async-done(((f32[4,256,256]{2,1,0:T(8,128)}), f32[4,256,256]{2,1,0:T(8,128)S(1)}, u32[]{:S(2)}, u32[]{:S(2)}) %all-to-all-start.1) | async-done | bytes 1048608 | tf_op jit(solution)/shard_map/all_to_all | solution.py:200
  64.0 1.1 fusion.1
  65.0 3.1 %collective-permute-start.2 = (f32[2,256,256]{2,1,0:T(8,128)}, f32[2,256,256]{2,1,0:T(8,128)}, u32[]{:S(2)}, u32[]{:S(2)}) collective-permute-start(f32[2,256,256]{2,1,0:T(8,128)} %get-tuple-element.36), channel_id=1, source_target_pairs={{0,4},{4,8},{8,12},{12,0},{1,5},{5,9},{9,13},{13,1},{2,6},{6,10},{... | collective-permute-start | bytes 1572872 | tf_op jit(solution)/shard_map/ppermute | solution.py:26
  68.1 4.0 %collective-permute-start.3 = (f32[2,256,256]{2,1,0:T(8,128)}, f32[2,256,256]{2,1,0:T(8,128)}, u32[]{:S(2)}, u32[]{:S(2)}) collective-permute-start(f32[2,256,256]{2,1,0:T(8,128)} %get-tuple-element.35), channel_id=1, source_target_pairs={{0,12},{4,0},{8,4},{12,8},{1,13},{5,1},{9,5},{13,9},{2,14},{6,2},{... | collective-permute-start | bytes 1572872 | tf_op jit(solution)/shard_map/ppermute | solution.py:26
  72.1 0.1 select_reduce_fusion.2.from_ref
  72.2 1.9 %collective-permute-start.9 = (f32[2,256,256]{2,1,0:T(8,128)}, f32[2,256,256]{2,1,0:T(8,128)}, u32[]{:S(2)}, u32[]{:S(2)}) collective-permute-start(f32[2,256,256]{2,1,0:T(8,128)} %get-tuple-element.35), channel_id=1, source_target_pairs={{0,4},{4,8},{8,12},{12,0},{1,5},{5,9},{9,13},{13,1},{2,6},{6,10},{... | collective-permute-start | bytes 1572872 | tf_op jit(solution)/shard_map/ppermute | solution.py:26
  74.1 5.1 %collective-permute-start.10 = (f32[2,256,256]{2,1,0:T(8,128)}, f32[2,256,256]{2,1,0:T(8,128)}, u32[]{:S(2)}, u32[]{:S(2)}) collective-permute-start(f32[2,256,256]{2,1,0:T(8,128)} %get-tuple-element.36), channel_id=1, source_target_pairs={{0,12},{4,0},{8,4},{12,8},{1,13},{5,1},{9,5},{13,9},{2,14},{6,2},{... | collective-permute-start | bytes 1572872 | tf_op jit(solution)/shard_map/ppermute | solution.py:26
  79.3 0.1 pad_add_fusion.2.quarter_ref
  79.4 0.0 collective-permute-done.4.refs_0_
  79.4 9.7 %collective-permute-start.5 = (f32[256,256]{1,0:T(8,128)S(1)}, f32[256,256]{1,0:T(8,128)}, u32[]{:S(2)}, u32[]{:S(2)}) collective-permute-start(f32[256,256]{1,0:T(8,128)S(1)} %get-tuple-element.25), channel_id=1, source_target_pairs={{0,3},{1,0},{2,1},{3,2},{4,7},{5,4},{6,5},{7,6},{8,11},{9,8},{10,9... | collective-permute-start | bytes 786440 | tf_op jit(solution)/shard_map/ppermute | solution.py:26
  89.1 0.1 pad_add_fusion.1.place_ref
  89.2 0.1 add.92
  89.2 0.0 copy-done.8
  89.3 0.0 collective-permute-done.2.refs_1_.refs_0_
  89.3 2.1 %collective-permute-start.7 = (f32[2,256,256]{2,1,0:T(8,128)}, f32[2,256,256]{2,1,0:T(8,128)S(1)}, u32[]{:S(2)}, u32[]{:S(2)}) collective-permute-start(f32[2,256,256]{2,1,0:T(8,128)} %collective-permute-done.2.refs_1_.refs_0_), channel_id=1, source_target_pairs={{0,4},{4,8},{8,12},{12,0},{1,5},{5,9},{9,13},{13,1},{2,6},{6,10},{... | collective-permute-start | bytes 1572872 | tf_op jit(solution)/shard_map/ppermute | solution.py:26
  91.3 0.0 collective-permute-done.3.refs_4_.refs_3_
  91.4 5.1 %collective-permute-start.8 = (f32[2,256,256]{2,1,0:T(8,128)}, f32[2,256,256]{2,1,0:T(8,128)S(1)}, u32[]{:S(2)}, u32[]{:S(2)}) collective-permute-start(f32[2,256,256]{2,1,0:T(8,128)} %collective-permute-done.3.refs_4_.refs_3_), channel_id=1, source_target_pairs={{0,12},{4,0},{8,4},{12,8},{1,13},{5,1},{9,5},{13,9},{2,14},{6,2},{... | collective-permute-start | bytes 1572872 | tf_op jit(solution)/shard_map/ppermute | solution.py:26
  96.5 0.0 collective-permute-done.5.refs_1_
  96.5 1.1 shard_map.57
  97.6 0.0 copy-done
  97.6 0.0 copy-done.2
  97.6 0.0 copy-done.4
  97.7 1.3 %shard_map.58 = f32[264,256]{1,0:T(8,128)S(1)} custom-call(s32[1]{0:T(128)} %bitcast.quarter_ref, s32[4]{0:T(128)S(1)} %select_reduce_fusion.2.from_ref, s32[4]{0:T(128)S(1)} %pad_add_fusion.1.place_ref, bf16[3,512,256]{2,1,0:T(8,128)(2,1)S(1)} %copy-done.2, bf16[3,512,256]{2,1,0:T(8,128)(2,1)S(1)} %copy-done.4, ...), custom_call_target="tpu_custom_call" | custom-call | flops 1000000000 | bytes 2000000 | tf_op jit(solution)/shard_map/pallas_call | solution.py:133
  99.0 3.1 %collective-permute-start.6 = (f32[264,256]{1,0:T(8,128)S(1)}, f32[264,256]{1,0:T(8,128)S(1)}, u32[]{:S(2)}, u32[]{:S(2)}) collective-permute-start(f32[264,256]{1,0:T(8,128)S(1)} %shard_map.58), channel_id=1, source_target_pairs={{0,256},{16,272},{32,288},{48,304},{64,320},{80,336},{96,352},{112... | collective-permute-start | bytes 811016 | tf_op jit(solution)/shard_map/ppermute | solution.py:196
  102.1 0.0 collective-permute-done.9.refs_2_.refs_1_
  102.1 0.0 collective-permute-done.10.refs_3_.refs_2_
  102.1 3.0 %shard_map.61 = f32[256,512]{1,0:T(8,128)S(1)} custom-call(s32[2]{0:T(128)S(1)} %pad_add_fusion.2.quarter_ref, s32[4]{0:T(128)S(1)} %select_reduce_fusion.2.from_ref, s32[4]{0:T(128)S(1)} %pad_add_fusion.1.place_ref, bf16[3,512,256]{2,1,0:T(8,128)(2,1)S(1)} %copy-done.2, bf16[3,512,256]{2,1,0:T(8,128)(2,1)S(1)} %copy-done.4, ...), custom_call_target="tpu_custom_call" | custom-call | flops 2000000000 | bytes 4000000 | tf_op jit(solution)/shard_map/pallas_call | solution.py:133
  105.1 2.7 %collective-permute-start.12 = (f32[256,512]{1,0:T(8,128)S(1)}, f32[256,512]{1,0:T(8,128)S(1)}, u32[]{:S(2)}, u32[]{:S(2)}) collective-permute-start(f32[256,512]{1,0:T(8,128)S(1)} %shard_map.61), channel_id=1, source_target_pairs={{0,256},{16,272},{32,288},{48,304},{64,320},{80,336},{96,352},{112... | collective-permute-start | bytes 1572872 | tf_op jit(solution)/shard_map/ppermute | solution.py:196
  107.9 0.0 collective-permute-done.7.refs_0_.refs_5_
  107.9 0.0 collective-permute-done.8.refs_1_.refs_6_
  107.9 1.4 %shard_map.59 = f32[256,256]{1,0:T(8,128)S(1)} custom-call(s32[1]{0:T(128)} %bitcast.3.quarter_ref, s32[4]{0:T(128)S(1)} %select_reduce_fusion.2.from_ref, s32[4]{0:T(128)S(1)} %pad_add_fusion.1.place_ref, bf16[3,512,256]{2,1,0:T(8,128)(2,1)S(1)} %copy-done.2, bf16[3,512,256]{2,1,0:T(8,128)(2,1)S(1)} %copy-done.4, ...), custom_call_target="tpu_custom_call" | custom-call | flops 1000000000 | bytes 2000000 | tf_op jit(solution)/shard_map/pallas_call | solution.py:133
  109.3 3.1 %collective-permute-start.11 = (f32[256,256]{1,0:T(8,128)S(1)}, f32[256,256]{1,0:T(8,128)S(1)}, u32[]{:S(2)}, u32[]{:S(2)}) collective-permute-start(f32[256,256]{1,0:T(8,128)S(1)} %shard_map.59), channel_id=1, source_target_pairs={{0,256},{16,272},{32,288},{48,304},{64,320},{80,336},{96,352},{112... | collective-permute-start | bytes 786440 | tf_op jit(solution)/shard_map/ppermute | solution.py:196
  112.4 4.2 %shard_map.60.refs_0_ = f32[256,1024]{1,0:T(8,128)S(1)} custom-call(s32[4]{0:T(128)S(1)} %get-tuple-element.28.quarter_ref, s32[4]{0:T(128)S(1)} %select_reduce_fusion.2.from_ref, s32[4]{0:T(128)S(1)} %pad_add_fusion.1.place_ref, bf16[3,512,256]{2,1,0:T(8,128)(2,1)S(1)} %copy-done.2, bf16[3,512,256]{2,1,0:T(8,128)(2,1)S(1)} %copy-done.4, ...), custom_call_target="tpu_custom_call" | custom-call | flops 4000000000 | bytes 8000000 | tf_op jit(solution)/shard_map/pallas_call | solution.py:133
  116.6 0.0 collective-permute-done.6.refs_1_
  116.6 0.2 select_reduce_fusion
  116.8 0.1 slice.24.slots_ref
  116.9 4.5 %collective-permute-done.12.refs_2_ = f32[256,512]{1,0:T(8,128)S(1)} collective-permute-done((f32[256,512]{1,0:T(8,128)S(1)}, f32[256,512]{1,0:T(8,128)S(1)}, u32[]{:S(2)}, u32[]{:S(2)}) %collective-permute-start.12) | collective-permute-done | bytes 524320 | tf_op jit(solution)/shard_map/ppermute | solution.py:196
  121.4 2.0 %shard_map.62.sum_ref = f32[256,1536]{1,0:T(8,128)} custom-call(s32[8]{0:T(128)S(1)} %get-tuple-element.31.mine_ref, s32[8]{0:T(128)S(1)} %get-tuple-element.32.other_ref, f32[256,1024]{1,0:T(8,128)S(1)} %shard_map.60.refs_0_, f32[264,256]{1,0:T(8,128)S(1)} %collective-permute-done.6.refs_1_, f32[256,512]{1,0:T(8,128)S(1)} %collective-permute-done.12.refs_2_), custom_call_target="tpu_custom_call" | custom-call | flops 2000000000 | bytes 4000000 | tf_op jit(solution)/shard_map/pallas_call | solution.py:157
  123.5 0.8 collective-permute-done.11.value_ref
  124.2 2.2 %shard_map.63 = f32[256,1536]{1,0:T(8,128)} custom-call(s32[2]{0:T(128)S(1)} %slice.24.slots_ref, f32[256,256]{1,0:T(8,128)S(1)} %collective-permute-done.11.value_ref, f32[256,1536]{1,0:T(8,128)} %shard_map.62.sum_ref), custom_call_target="tpu_custom_call", output_to_operand_aliasing={{}: (2, {})} | custom-call | flops 1000000000 | bytes 2000000 | tf_op jit(solution)/shard_map/pallas_call | solution.py:174
  (9 shorter events, 0.0 us)
Async XLA Ops:
  0.0 1.2 copy-start.5
  1.2 0.7 copy-start.6
  3.5 12.7 %copy-start.7 = (s32[1,4]{1,0:T(1,128)S(1)}, s32[1,4]{1,0:T(1,128)}, u32[]{:S(2)}) copy-start(s32[1,4]{1,0:T(1,128)} %param.8) | copy-start | bytes 52
  3.5 19.8 %all-to-all-start = ((f32[4,256,256]{2,1,0:T(8,128)}), f32[4,256,256]{2,1,0:T(8,128)}, u32[]{:S(2)}, u32[]{:S(2)}) async-start(f32[4,256,256]{2,1,0:T(8,128)} %bitcast.11), calls=%async_computation | async-start | bytes 2097152 | tf_op jit(solution)/shard_map/all_to_all | solution.py:199
  8.0 25.3 %collective-permute-start = (f32[512,256]{1,0:T(8,128)S(1)}, f32[512,256]{1,0:T(8,128)S(1)}, u32[]{:S(2)}, u32[]{:S(2)}) collective-permute-start(f32[512,256]{1,0:T(8,128)S(1)} %get-tuple-element.18.refs_0_), channel_id=1, source_target_pairs={{0,1},{1,2},{2,3},{3,0},{4,5},{5,6},{6,7},{7,4},{8,9},{9,10},{10,1... | collective-permute-start | bytes 1572872 | tf_op jit(solution)/shard_map/ppermute | solution.py:26
  12.4 40.1 %collective-permute-start.1 = (f32[512,256]{1,0:T(8,128)S(1)}, f32[512,256]{1,0:T(8,128)S(1)}, u32[]{:S(2)}, u32[]{:S(2)}) collective-permute-start(f32[512,256]{1,0:T(8,128)S(1)} %get-tuple-element.18.refs_0_), channel_id=1, source_target_pairs={{0,3},{1,0},{2,1},{3,2},{4,7},{5,4},{6,5},{7,6},{8,11},{9,8},{10,9... | collective-permute-start | bytes 1572872 | tf_op jit(solution)/shard_map/ppermute | solution.py:26
  23.3 40.6 %all-to-all-start.1 = ((f32[4,256,256]{2,1,0:T(8,128)}), f32[4,256,256]{2,1,0:T(8,128)S(1)}, u32[]{:S(2)}, u32[]{:S(2)}) async-start(f32[4,256,256]{2,1,0:T(8,128)} %all-to-all-done), calls=%async_computation.1 | async-start | bytes 2097152 | tf_op jit(solution)/shard_map/all_to_all | solution.py:200
  54.0 0.9 copy-start.1
  54.8 0.9 copy-start.3
  55.7 33.5 %copy-start.8 = (s32[1,12]{1,0:T(1,128)S(1)}, s32[1,12]{1,0:T(1,128)}, u32[]{:S(2)}) copy-start(s32[1,12]{1,0:T(1,128)} %param.9) | copy-start | bytes 148
  55.7 41.9 %copy-start = (f32[512,1024]{1,0:T(8,128)S(1)}, f32[512,1024]{1,0:T(8,128)}, u32[]{:S(2)}) copy-start(f32[512,1024]{1,0:T(8,128)} %front_ref.7) | copy-start | bytes 6291460
  55.7 23.6 %collective-permute-start.4 = (f32[256,256]{1,0:T(8,128)}, f32[256,256]{1,0:T(8,128)}, u32[]{:S(2)}, u32[]{:S(2)}) collective-permute-start(f32[256,256]{1,0:T(8,128)} %get-tuple-element.22), channel_id=1, source_target_pairs={{0,1},{1,2},{2,3},{3,0},{4,5},{5,6},{6,7},{7,4},{8,9},{9,10},{10,1... | collective-permute-start | bytes 786440 | tf_op jit(solution)/shard_map/ppermute | solution.py:26
  65.0 24.2 %collective-permute-start.2 = (f32[2,256,256]{2,1,0:T(8,128)}, f32[2,256,256]{2,1,0:T(8,128)}, u32[]{:S(2)}, u32[]{:S(2)}) collective-permute-start(f32[2,256,256]{2,1,0:T(8,128)} %get-tuple-element.36), channel_id=1, source_target_pairs={{0,4},{4,8},{8,12},{12,0},{1,5},{5,9},{9,13},{13,1},{2,6},{6,10},{... | collective-permute-start | bytes 1572872 | tf_op jit(solution)/shard_map/ppermute | solution.py:26
  68.1 23.2 %collective-permute-start.3 = (f32[2,256,256]{2,1,0:T(8,128)}, f32[2,256,256]{2,1,0:T(8,128)}, u32[]{:S(2)}, u32[]{:S(2)}) collective-permute-start(f32[2,256,256]{2,1,0:T(8,128)} %get-tuple-element.35), channel_id=1, source_target_pairs={{0,12},{4,0},{8,4},{12,8},{1,13},{5,1},{9,5},{13,9},{2,14},{6,2},{... | collective-permute-start | bytes 1572872 | tf_op jit(solution)/shard_map/ppermute | solution.py:26
  72.2 29.9 %collective-permute-start.9 = (f32[2,256,256]{2,1,0:T(8,128)}, f32[2,256,256]{2,1,0:T(8,128)}, u32[]{:S(2)}, u32[]{:S(2)}) collective-permute-start(f32[2,256,256]{2,1,0:T(8,128)} %get-tuple-element.35), channel_id=1, source_target_pairs={{0,4},{4,8},{8,12},{12,0},{1,5},{5,9},{9,13},{13,1},{2,6},{6,10},{... | collective-permute-start | bytes 1572872 | tf_op jit(solution)/shard_map/ppermute | solution.py:26
  74.1 28.0 %collective-permute-start.10 = (f32[2,256,256]{2,1,0:T(8,128)}, f32[2,256,256]{2,1,0:T(8,128)}, u32[]{:S(2)}, u32[]{:S(2)}) collective-permute-start(f32[2,256,256]{2,1,0:T(8,128)} %get-tuple-element.36), channel_id=1, source_target_pairs={{0,12},{4,0},{8,4},{12,8},{1,13},{5,1},{9,5},{13,9},{2,14},{6,2},{... | collective-permute-start | bytes 1572872 | tf_op jit(solution)/shard_map/ppermute | solution.py:26
  79.4 17.1 %collective-permute-start.5 = (f32[256,256]{1,0:T(8,128)S(1)}, f32[256,256]{1,0:T(8,128)}, u32[]{:S(2)}, u32[]{:S(2)}) collective-permute-start(f32[256,256]{1,0:T(8,128)S(1)} %get-tuple-element.25), channel_id=1, source_target_pairs={{0,3},{1,0},{2,1},{3,2},{4,7},{5,4},{6,5},{7,6},{8,11},{9,8},{10,9... | collective-permute-start | bytes 786440 | tf_op jit(solution)/shard_map/ppermute | solution.py:26
  89.2 8.4 %copy-start.2 = (bf16[3,512,256]{2,1,0:T(8,128)(2,1)S(1)}, bf16[3,512,256]{2,1,0:T(8,128)(2,1)}, u32[]{:S(2)}) copy-start(bf16[3,512,256]{2,1,0:T(8,128)(2,1)} %copy-done.1) | copy-start | bytes 2359300
  89.2 8.4 %copy-start.4 = (bf16[3,512,256]{2,1,0:T(8,128)(2,1)S(1)}, bf16[3,512,256]{2,1,0:T(8,128)(2,1)}, u32[]{:S(2)}) copy-start(bf16[3,512,256]{2,1,0:T(8,128)(2,1)} %copy-done.3) | copy-start | bytes 2359300
  89.3 18.6 %collective-permute-start.7 = (f32[2,256,256]{2,1,0:T(8,128)}, f32[2,256,256]{2,1,0:T(8,128)S(1)}, u32[]{:S(2)}, u32[]{:S(2)}) collective-permute-start(f32[2,256,256]{2,1,0:T(8,128)} %collective-permute-done.2.refs_1_.refs_0_), channel_id=1, source_target_pairs={{0,4},{4,8},{8,12},{12,0},{1,5},{5,9},{9,13},{13,1},{2,6},{6,10},{... | collective-permute-start | bytes 1572872 | tf_op jit(solution)/shard_map/ppermute | solution.py:26
  91.4 16.5 %collective-permute-start.8 = (f32[2,256,256]{2,1,0:T(8,128)}, f32[2,256,256]{2,1,0:T(8,128)S(1)}, u32[]{:S(2)}, u32[]{:S(2)}) collective-permute-start(f32[2,256,256]{2,1,0:T(8,128)} %collective-permute-done.3.refs_4_.refs_3_), channel_id=1, source_target_pairs={{0,12},{4,0},{8,4},{12,8},{1,13},{5,1},{9,5},{13,9},{2,14},{6,2},{... | collective-permute-start | bytes 1572872 | tf_op jit(solution)/shard_map/ppermute | solution.py:26
  99.0 17.6 %collective-permute-start.6 = (f32[264,256]{1,0:T(8,128)S(1)}, f32[264,256]{1,0:T(8,128)S(1)}, u32[]{:S(2)}, u32[]{:S(2)}) collective-permute-start(f32[264,256]{1,0:T(8,128)S(1)} %shard_map.58), channel_id=1, source_target_pairs={{0,256},{16,272},{32,288},{48,304},{64,320},{80,336},{96,352},{112... | collective-permute-start | bytes 811016 | tf_op jit(solution)/shard_map/ppermute | solution.py:196
  105.1 16.3 %collective-permute-start.12 = (f32[256,512]{1,0:T(8,128)S(1)}, f32[256,512]{1,0:T(8,128)S(1)}, u32[]{:S(2)}, u32[]{:S(2)}) collective-permute-start(f32[256,512]{1,0:T(8,128)S(1)} %shard_map.61), channel_id=1, source_target_pairs={{0,256},{16,272},{32,288},{48,304},{64,320},{80,336},{96,352},{112... | collective-permute-start | bytes 1572872 | tf_op jit(solution)/shard_map/ppermute | solution.py:196
  109.3 15.0 %collective-permute-start.11 = (f32[256,256]{1,0:T(8,128)S(1)}, f32[256,256]{1,0:T(8,128)S(1)}, u32[]{:S(2)}, u32[]{:S(2)}) collective-permute-start(f32[256,256]{1,0:T(8,128)S(1)} %shard_map.59), channel_id=1, source_target_pairs={{0,256},{16,272},{32,288},{48,304},{64,320},{80,336},{96,352},{112... | collective-permute-start | bytes 786440 | tf_op jit(solution)/shard_map/ppermute | solution.py:196

commit v3 on v2

--- a/solution.py
+++ b/solution.py
@@ -206,6 +206,7 @@
     ).astype(jnp.int32)
     *near, low, high = split_window(to, 3, 60, window, before, after, forward=True)
     mine = after_all(mine, low)
+    low, high = after_all(low, mine), after_all(high, mine)
     far_low, far_high = shift(low, "col", 1), shift(high, "col", -1)
     lower, upper_half = mine[: n_col // 2], mine[n_col // 2 :]
     b_low, a_high = shift(lower, "row", 1), shift(upper_half, "row", -1)

time: 127 us -> 132 us (1.039)
  waiting for transfers between devices: 37.2 us -> 40.8 us
    ppermute x3, waiting for transfers between devices: 5.26 us -> 7.23 us  [body(): to_sibling = lambda v: lax.ppermute(v, 'leaf', pairs)]
    ppermute x10, waiting for transfers between devices: 22.1 us -> 23.7 us  [shift(): lax.ppermute(value, axis, [(i, (i + by) % size) for i in range(size)])]
  transfers between devices with their start and end apart: 15 -> 15, of which waited for: 6 -> 8; matrix products, arithmetic and copies ran while one was open for 1% -> 1% of each run, Pallas kernels for 11% -> 11%
where the time goes in v3:
time: 132 us; the launch traced here: 131 us
  starting transfers between devices  65.9 us (50%)
  waiting for transfers between devices  40.8 us (31%)
  Pallas kernels  18.3 us (14%)
  local copies, waits for them, and re-layouts  4.93 us (4%)
    ppermute x10, starting transfers between devices, shift(): lax.ppermute(value, axis, [(i, (i + by) % size) for i in range(size)])  45.3 us
    ppermute x10, waiting for transfers between devices, shift(): lax.ppermute(value, axis, [(i, (i + by) % size) for i in range(size)])  23.7 us
    pallas_call x4, Pallas kernels, update(): pl.pallas_call(functools.partial(update_kernel, counts, firsts, more), ou...  9.93 us
    ppermute x3, starting transfers between devices, body(): to_sibling = lambda v: lax.ppermute(v, 'leaf', pairs)  9.07 us
    ppermute x3, waiting for transfers between devices, body(): to_sibling = lambda v: lax.ppermute(v, 'leaf', pairs)  7.23 us
    all_to_all x1, starting transfers between devices, body(): lax.all_to_all(by_row, 'col', 0, 0, tiled=True)  7.09 us
    all_to_all x1, waiting for transfers between devices, body(): by_row = lax.all_to_all(masked, 'row', 0, 0, tiled=True)  7.07 us
    all_to_all x1, starting transfers between devices, body(): by_row = lax.all_to_all(masked, 'row', 0, 0, tiled=True)  4.42 us
  transfers between devices with their start and end apart: 15, of which 8 were waited for; matrix products, arithmetic and copies ran while one was open for 1% of the time, Pallas kernels for 11%

profile of v3, /device:TPU:448, one launch (start us, length us, event | category | flops | bytes accessed | tf_op | source)
XLA Modules:
  0.0 131.0 jit_solution(7721175281682276452)
XLA Ops:
  0.0 0.0 copy-start.5
  0.0 1.2 copy-done.5
  1.2 0.0 copy-start.6
  1.2 0.7 copy-done.6
  1.9 1.6 %shard_map.55 = (f32[1024,256]{1,0:T(8,128)}, f32[512,256]{1,0:T(8,128)S(1)}) custom-call(s32[2,8]{1,0:T(2,128)S(1)} %bitcast.24, f32[1024,256]{1,0:T(8,128)S(1)} %copy-done.5), custom_call_target="tpu_custom_call" | custom-call | flops 1500000000 | bytes 3000000 | tf_op jit(solution)/shard_map/pallas_call | solution.py:41
  3.5 0.0 copy-start.7
  3.5 4.4 %all-to-all-start = ((f32[4,256,256]{2,1,0:T(8,128)}), f32[4,256,256]{2,1,0:T(8,128)}, u32[]{:S(2)}, u32[]{:S(2)}) async-start(f32[4,256,256]{2,1,0:T(8,128)} %bitcast.11), calls=%async_computation | async-start | bytes 2097152 | tf_op jit(solution)/shard_map/all_to_all | solution.py:199
  8.0 4.5 %collective-permute-start = (f32[512,256]{1,0:T(8,128)S(1)}, f32[512,256]{1,0:T(8,128)S(1)}, u32[]{:S(2)}, u32[]{:S(2)}) collective-permute-start(f32[512,256]{1,0:T(8,128)S(1)} %get-tuple-element.20.refs_0_), channel_id=1, source_target_pairs={{0,1},{1,2},{2,3},{3,0},{4,5},{5,6},{6,7},{7,4},{8,9},{9,10},{10,1... | collective-permute-start | bytes 1572872 | tf_op jit(solution)/shard_map/ppermute | solution.py:26
  12.4 3.6 %collective-permute-start.1 = (f32[512,256]{1,0:T(8,128)S(1)}, f32[512,256]{1,0:T(8,128)S(1)}, u32[]{:S(2)}, u32[]{:S(2)}) collective-permute-start(f32[512,256]{1,0:T(8,128)S(1)} %get-tuple-element.20.refs_0_), channel_id=1, source_target_pairs={{0,3},{1,0},{2,1},{3,2},{4,7},{5,4},{6,5},{7,6},{8,11},{9,8},{10,9... | collective-permute-start | bytes 1572872 | tf_op jit(solution)/shard_map/ppermute | solution.py:26
  16.1 0.1 broadcast_multiply_fusion
  16.2 0.0 copy-done.7
  16.2 0.1 iota_add_fusion
  16.3 7.1 %all-to-all-done = f32[4,256,256]{2,1,0:T(8,128)} async-done(((f32[4,256,256]{2,1,0:T(8,128)}), f32[4,256,256]{2,1,0:T(8,128)}, u32[]{:S(2)}, u32[]{:S(2)}) %all-to-all-start) | async-done | bytes 1048608 | tf_op jit(solution)/shard_map/all_to_all | solution.py:199
  23.3 7.1 %all-to-all-start.1 = ((f32[4,256,256]{2,1,0:T(8,128)}), f32[4,256,256]{2,1,0:T(8,128)S(1)}, u32[]{:S(2)}, u32[]{:S(2)}) async-start(f32[4,256,256]{2,1,0:T(8,128)} %all-to-all-done), calls=%async_computation.1 | async-start | bytes 2097152 | tf_op jit(solution)/shard_map/all_to_all | solution.py:200
  30.4 2.8 %collective-permute-done.refs_1_ = f32[512,256]{1,0:T(8,128)S(1)} collective-permute-done((f32[512,256]{1,0:T(8,128)S(1)}, f32[512,256]{1,0:T(8,128)S(1)}, u32[]{:S(2)}, u32[]{:S(2)}) %collective-permute-start) | collective-permute-done | bytes 524320 | tf_op jit(solution)/shard_map/ppermute | solution.py:26
  33.3 19.3 %collective-permute-done.1.refs_2_ = f32[512,256]{1,0:T(8,128)S(1)} collective-permute-done((f32[512,256]{1,0:T(8,128)S(1)}, f32[512,256]{1,0:T(8,128)S(1)}, u32[]{:S(2)}, u32[]{:S(2)}) %collective-permute-start.1) | collective-permute-done | bytes 524320 | tf_op jit(solution)/shard_map/ppermute | solution.py:26
  52.6 1.4 %shard_map.56 = (bf16[3,512,256]{2,1,0:T(8,128)(2,1)S(1)}, bf16[3,512,256]{2,1,0:T(8,128)(2,1)S(1)}, f32[256,256]{1,0:T(8,128)}, f32[256,256]{1,0:T(8,128)S(1)}) custom-call(s32[4]{0:T(128)S(1)} %compare_select_fusion.to_ref, f32[512,256]{1,0:T(8,128)S(1)} %get-tuple-element.20.refs_0_, f32[512,256]{1,0:T(8,128)S(1)} %collective-permute-done.refs_1_, ...), custom_call_target="tpu_custom_call" | custom-call | flops 60000002048 | bytes 120000000 | tf_op jit(solution)/shard_map/pallas_call | solution.py:82
  53.9 0.0 copy-start.1
  53.9 0.9 copy-done.1
  54.8 0.0 copy-start.3
  54.8 0.9 copy-done.3
  55.7 0.0 copy-start.8
  55.7 2.9 %all-to-all-done.1.refs_1_.refs_0_ = f32[4,256,256]{2,1,0:T(8,128)S(1)} async-done(((f32[4,256,256]{2,1,0:T(8,128)}), f32[4,256,256]{2,1,0:T(8,128)S(1)}, u32[]{:S(2)}, u32[]{:S(2)}) %all-to-all-start.1) | async-done | bytes 1048608 | tf_op jit(solution)/shard_map/all_to_all | solution.py:200
  58.6 0.0 copy-start
  58.6 1.1 fusion.1
  59.7 4.2 %collective-permute-start.2 = (f32[2,256,256]{2,1,0:T(8,128)}, f32[2,256,256]{2,1,0:T(8,128)}, u32[]{:S(2)}, u32[]{:S(2)}) collective-permute-start(f32[2,256,256]{2,1,0:T(8,128)} %get-tuple-element.40), channel_id=1, source_target_pairs={{0,4},{4,8},{8,12},{12,0},{1,5},{5,9},{9,13},{13,1},{2,6},{6,10},{... | collective-permute-start | bytes 1572872 | tf_op jit(solution)/shard_map/ppermute | solution.py:26
  63.9 3.1 %collective-permute-start.3 = (f32[2,256,256]{2,1,0:T(8,128)}, f32[2,256,256]{2,1,0:T(8,128)}, u32[]{:S(2)}, u32[]{:S(2)}) collective-permute-start(f32[2,256,256]{2,1,0:T(8,128)} %get-tuple-element.39), channel_id=1, source_target_pairs={{0,12},{4,0},{8,4},{12,8},{1,13},{5,1},{9,5},{13,9},{2,14},{6,2},{... | collective-permute-start | bytes 1572872 | tf_op jit(solution)/shard_map/ppermute | solution.py:26
  67.1 5.9 %collective-permute-start.4 = (f32[256,256]{1,0:T(8,128)}, f32[256,256]{1,0:T(8,128)}, u32[]{:S(2)}, u32[]{:S(2)}) collective-permute-start(f32[256,256]{1,0:T(8,128)} %get-tuple-element.27), channel_id=1, source_target_pairs={{0,1},{1,2},{2,3},{3,0},{4,5},{5,6},{6,7},{7,4},{8,9},{9,10},{10,1... | collective-permute-start | bytes 786440 | tf_op jit(solution)/shard_map/ppermute | solution.py:26
  73.0 0.1 select_reduce_fusion.2.from_ref
  73.1 2.7 %collective-permute-start.9 = (f32[2,256,256]{2,1,0:T(8,128)}, f32[2,256,256]{2,1,0:T(8,128)}, u32[]{:S(2)}, u32[]{:S(2)}) collective-permute-start(f32[2,256,256]{2,1,0:T(8,128)} %get-tuple-element.39), channel_id=1, source_target_pairs={{0,4},{4,8},{8,12},{12,0},{1,5},{5,9},{9,13},{13,1},{2,6},{6,10},{... | collective-permute-start | bytes 1572872 | tf_op jit(solution)/shard_map/ppermute | solution.py:26
  75.7 4.4 %collective-permute-start.10 = (f32[2,256,256]{2,1,0:T(8,128)}, f32[2,256,256]{2,1,0:T(8,128)}, u32[]{:S(2)}, u32[]{:S(2)}) collective-permute-start(f32[2,256,256]{2,1,0:T(8,128)} %get-tuple-element.40), channel_id=1, source_target_pairs={{0,12},{4,0},{8,4},{12,8},{1,13},{5,1},{9,5},{13,9},{2,14},{6,2},{... | collective-permute-start | bytes 1572872 | tf_op jit(solution)/shard_map/ppermute | solution.py:26
  80.1 0.1 pad_add_fusion.2.quarter_ref
  80.2 0.7 collective-permute-done.4.refs_0_
  80.9 9.8 %collective-permute-start.5 = (f32[256,256]{1,0:T(8,128)S(1)}, f32[256,256]{1,0:T(8,128)}, u32[]{:S(2)}, u32[]{:S(2)}) collective-permute-start(f32[256,256]{1,0:T(8,128)S(1)} %get-tuple-element.29), channel_id=1, source_target_pairs={{0,3},{1,0},{2,1},{3,2},{4,7},{5,4},{6,5},{7,6},{8,11},{9,8},{10,9... | collective-permute-start | bytes 786440 | tf_op jit(solution)/shard_map/ppermute | solution.py:26
  90.7 0.1 pad_add_fusion.1.place_ref
  90.7 0.1 add.92
  90.8 0.0 copy-done.8
  90.8 0.0 collective-permute-done.2.refs_1_.refs_0_
  90.9 2.2 %collective-permute-start.7 = (f32[2,256,256]{2,1,0:T(8,128)}, f32[2,256,256]{2,1,0:T(8,128)S(1)}, u32[]{:S(2)}, u32[]{:S(2)}) collective-permute-start(f32[2,256,256]{2,1,0:T(8,128)} %collective-permute-done.2.refs_1_.refs_0_), channel_id=1, source_target_pairs={{0,4},{4,8},{8,12},{12,0},{1,5},{5,9},{9,13},{13,1},{2,6},{6,10},{... | collective-permute-start | bytes 1572872 | tf_op jit(solution)/shard_map/ppermute | solution.py:26
  93.1 0.0 collective-permute-done.3.refs_4_.refs_3_
  93.1 5.0 %collective-permute-start.8 = (f32[2,256,256]{2,1,0:T(8,128)}, f32[2,256,256]{2,1,0:T(8,128)S(1)}, u32[]{:S(2)}, u32[]{:S(2)}) collective-permute-start(f32[2,256,256]{2,1,0:T(8,128)} %collective-permute-done.3.refs_4_.refs_3_), channel_id=1, source_target_pairs={{0,12},{4,0},{8,4},{12,8},{1,13},{5,1},{9,5},{13,9},{2,14},{6,2},{... | collective-permute-start | bytes 1572872 | tf_op jit(solution)/shard_map/ppermute | solution.py:26
  98.1 0.9 collective-permute-done.5.refs_1_
  98.9 1.1 shard_map.57
  100.0 0.0 copy-done
  100.1 0.0 copy-done.2
  100.1 0.0 copy-done.4
  100.1 1.3 %shard_map.58 = f32[264,256]{1,0:T(8,128)S(1)} custom-call(s32[1]{0:T(128)} %bitcast.quarter_ref, s32[4]{0:T(128)S(1)} %select_reduce_fusion.2.from_ref, s32[4]{0:T(128)S(1)} %pad_add_fusion.1.place_ref, bf16[3,512,256]{2,1,0:T(8,128)(2,1)S(1)} %copy-done.2, bf16[3,512,256]{2,1,0:T(8,128)(2,1)S(1)} %copy-done.4, ...), custom_call_target="tpu_custom_call" | custom-call | flops 1000000000 | bytes 2000000 | tf_op jit(solution)/shard_map/pallas_call | solution.py:133
  101.4 3.2 %collective-permute-start.6 = (f32[264,256]{1,0:T(8,128)S(1)}, f32[264,256]{1,0:T(8,128)S(1)}, u32[]{:S(2)}, u32[]{:S(2)}) collective-permute-start(f32[264,256]{1,0:T(8,128)S(1)} %shard_map.58), channel_id=1, source_target_pairs={{0,256},{16,272},{32,288},{48,304},{64,320},{80,336},{96,352},{112... | collective-permute-start | bytes 811016 | tf_op jit(solution)/shard_map/ppermute | solution.py:196
  104.7 0.0 collective-permute-done.9.refs_2_.refs_1_
  104.7 0.0 collective-permute-done.10.refs_3_.refs_2_
  104.7 3.0 %shard_map.61 = f32[256,512]{1,0:T(8,128)S(1)} custom-call(s32[2]{0:T(128)S(1)} %pad_add_fusion.2.quarter_ref, s32[4]{0:T(128)S(1)} %select_reduce_fusion.2.from_ref, s32[4]{0:T(128)S(1)} %pad_add_fusion.1.place_ref, bf16[3,512,256]{2,1,0:T(8,128)(2,1)S(1)} %copy-done.2, bf16[3,512,256]{2,1,0:T(8,128)(2,1)S(1)} %copy-done.4, ...), custom_call_target="tpu_custom_call" | custom-call | flops 2000000000 | bytes 4000000 | tf_op jit(solution)/shard_map/pallas_call | solution.py:133
  107.7 2.6 %collective-permute-start.12 = (f32[256,512]{1,0:T(8,128)S(1)}, f32[256,512]{1,0:T(8,128)S(1)}, u32[]{:S(2)}, u32[]{:S(2)}) collective-permute-start(f32[256,512]{1,0:T(8,128)S(1)} %shard_map.61), channel_id=1, source_target_pairs={{0,256},{16,272},{32,288},{48,304},{64,320},{80,336},{96,352},{112... | collective-permute-start | bytes 1572872 | tf_op jit(solution)/shard_map/ppermute | solution.py:196
  110.3 0.0 collective-permute-done.7.refs_0_.refs_5_
  110.3 0.0 collective-permute-done.8.refs_1_.refs_6_
  110.3 1.4 %shard_map.59 = f32[256,256]{1,0:T(8,128)S(1)} custom-call(s32[1]{0:T(128)} %bitcast.3.quarter_ref, s32[4]{0:T(128)S(1)} %select_reduce_fusion.2.from_ref, s32[4]{0:T(128)S(1)} %pad_add_fusion.1.place_ref, bf16[3,512,256]{2,1,0:T(8,128)(2,1)S(1)} %copy-done.2, bf16[3,512,256]{2,1,0:T(8,128)(2,1)S(1)} %copy-done.4, ...), custom_call_target="tpu_custom_call" | custom-call | flops 1000000000 | bytes 2000000 | tf_op jit(solution)/shard_map/pallas_call | solution.py:133
  111.7 3.2 %collective-permute-start.11 = (f32[256,256]{1,0:T(8,128)S(1)}, f32[256,256]{1,0:T(8,128)S(1)}, u32[]{:S(2)}, u32[]{:S(2)}) collective-permute-start(f32[256,256]{1,0:T(8,128)S(1)} %shard_map.59), channel_id=1, source_target_pairs={{0,256},{16,272},{32,288},{48,304},{64,320},{80,336},{96,352},{112... | collective-permute-start | bytes 786440 | tf_op jit(solution)/shard_map/ppermute | solution.py:196
  114.9 4.2 %shard_map.60.refs_0_ = f32[256,1024]{1,0:T(8,128)S(1)} custom-call(s32[4]{0:T(128)S(1)} %get-tuple-element.32.quarter_ref, s32[4]{0:T(128)S(1)} %select_reduce_fusion.2.from_ref, s32[4]{0:T(128)S(1)} %pad_add_fusion.1.place_ref, bf16[3,512,256]{2,1,0:T(8,128)(2,1)S(1)} %copy-done.2, bf16[3,512,256]{2,1,0:T(8,128)(2,1)S(1)} %copy-done.4, ...), custom_call_target="tpu_custom_call" | custom-call | flops 4000000000 | bytes 8000000 | tf_op jit(solution)/shard_map/pallas_call | solution.py:133
  119.2 0.0 collective-permute-done.6.refs_1_
  119.2 0.2 select_reduce_fusion
  119.4 0.1 slice.24.slots_ref
  119.5 4.9 %collective-permute-done.12.refs_2_ = f32[256,512]{1,0:T(8,128)S(1)} collective-permute-done((f32[256,512]{1,0:T(8,128)S(1)}, f32[256,512]{1,0:T(8,128)S(1)}, u32[]{:S(2)}, u32[]{:S(2)}) %collective-permute-start.12) | collective-permute-done | bytes 524320 | tf_op jit(solution)/shard_map/ppermute | solution.py:196
  124.4 2.1 %shard_map.62.sum_ref = f32[256,1536]{1,0:T(8,128)} custom-call(s32[8]{0:T(128)S(1)} %get-tuple-element.35.mine_ref, s32[8]{0:T(128)S(1)} %get-tuple-element.36.other_ref, f32[256,1024]{1,0:T(8,128)S(1)} %shard_map.60.refs_0_, f32[264,256]{1,0:T(8,128)S(1)} %collective-permute-done.6.refs_1_, f32[256,512]{1,0:T(8,128)S(1)} %collective-permute-done.12.refs_2_), custom_call_target="tpu_custom_call" | custom-call | flops 2000000000 | bytes 4000000 | tf_op jit(solution)/shard_map/pallas_call | solution.py:157
  126.4 2.3 %collective-permute-done.11.value_ref = f32[256,256]{1,0:T(8,128)S(1)} collective-permute-done((f32[256,256]{1,0:T(8,128)S(1)}, f32[256,256]{1,0:T(8,128)S(1)}, u32[]{:S(2)}, u32[]{:S(2)}) %collective-permute-start.11) | collective-permute-done | bytes 262176 | tf_op jit(solution)/shard_map/ppermute | solution.py:196
  128.7 2.2 %shard_map.63 = f32[256,1536]{1,0:T(8,128)} custom-call(s32[2]{0:T(128)S(1)} %slice.24.slots_ref, f32[256,256]{1,0:T(8,128)S(1)} %collective-permute-done.11.value_ref, f32[256,1536]{1,0:T(8,128)} %shard_map.62.sum_ref), custom_call_target="tpu_custom_call", output_to_operand_aliasing={{}: (2, {})} | custom-call | flops 1000000000 | bytes 2000000 | tf_op jit(solution)/shard_map/pallas_call | solution.py:174
  (9 shorter events, 0.0 us)
Async XLA Ops:
  0.0 1.2 copy-start.5
  1.2 0.7 copy-start.6
  3.5 12.7 %copy-start.7 = (s32[1,4]{1,0:T(1,128)S(1)}, s32[1,4]{1,0:T(1,128)}, u32[]{:S(2)}) copy-start(s32[1,4]{1,0:T(1,128)} %param.8) | copy-start | bytes 52
  3.5 19.8 %all-to-all-start = ((f32[4,256,256]{2,1,0:T(8,128)}), f32[4,256,256]{2,1,0:T(8,128)}, u32[]{:S(2)}, u32[]{:S(2)}) async-start(f32[4,256,256]{2,1,0:T(8,128)} %bitcast.11), calls=%async_computation | async-start | bytes 2097152 | tf_op jit(solution)/shard_map/all_to_all | solution.py:199
  8.0 25.3 %collective-permute-start = (f32[512,256]{1,0:T(8,128)S(1)}, f32[512,256]{1,0:T(8,128)S(1)}, u32[]{:S(2)}, u32[]{:S(2)}) collective-permute-start(f32[512,256]{1,0:T(8,128)S(1)} %get-tuple-element.20.refs_0_), channel_id=1, source_target_pairs={{0,1},{1,2},{2,3},{3,0},{4,5},{5,6},{6,7},{7,4},{8,9},{9,10},{10,1... | collective-permute-start | bytes 1572872 | tf_op jit(solution)/shard_map/ppermute | solution.py:26
  12.4 40.1 %collective-permute-start.1 = (f32[512,256]{1,0:T(8,128)S(1)}, f32[512,256]{1,0:T(8,128)S(1)}, u32[]{:S(2)}, u32[]{:S(2)}) collective-permute-start(f32[512,256]{1,0:T(8,128)S(1)} %get-tuple-element.20.refs_0_), channel_id=1, source_target_pairs={{0,3},{1,0},{2,1},{3,2},{4,7},{5,4},{6,5},{7,6},{8,11},{9,8},{10,9... | collective-permute-start | bytes 1572872 | tf_op jit(solution)/shard_map/ppermute | solution.py:26
  23.3 35.3 %all-to-all-start.1 = ((f32[4,256,256]{2,1,0:T(8,128)}), f32[4,256,256]{2,1,0:T(8,128)S(1)}, u32[]{:S(2)}, u32[]{:S(2)}) async-start(f32[4,256,256]{2,1,0:T(8,128)} %all-to-all-done), calls=%async_computation.1 | async-start | bytes 2097152 | tf_op jit(solution)/shard_map/all_to_all | solution.py:200
  53.9 0.9 copy-start.1
  54.8 0.9 copy-start.3
  55.7 35.1 %copy-start.8 = (s32[1,12]{1,0:T(1,128)S(1)}, s32[1,12]{1,0:T(1,128)}, u32[]{:S(2)}) copy-start(s32[1,12]{1,0:T(1,128)} %param.9) | copy-start | bytes 148
  58.6 41.4 %copy-start = (f32[512,1024]{1,0:T(8,128)S(1)}, f32[512,1024]{1,0:T(8,128)}, u32[]{:S(2)}) copy-start(f32[512,1024]{1,0:T(8,128)} %front_ref.7) | copy-start | bytes 6291460
  59.7 31.2 %collective-permute-start.2 = (f32[2,256,256]{2,1,0:T(8,128)}, f32[2,256,256]{2,1,0:T(8,128)}, u32[]{:S(2)}, u32[]{:S(2)}) collective-permute-start(f32[2,256,256]{2,1,0:T(8,128)} %get-tuple-element.40), channel_id=1, source_target_pairs={{0,4},{4,8},{8,12},{12,0},{1,5},{5,9},{9,13},{13,1},{2,6},{6,10},{... | collective-permute-start | bytes 1572872 | tf_op jit(solution)/shard_map/ppermute | solution.py:26
  63.9 29.2 %collective-permute-start.3 = (f32[2,256,256]{2,1,0:T(8,128)}, f32[2,256,256]{2,1,0:T(8,128)}, u32[]{:S(2)}, u32[]{:S(2)}) collective-permute-start(f32[2,256,256]{2,1,0:T(8,128)} %get-tuple-element.39), channel_id=1, source_target_pairs={{0,12},{4,0},{8,4},{12,8},{1,13},{5,1},{9,5},{13,9},{2,14},{6,2},{... | collective-permute-start | bytes 1572872 | tf_op jit(solution)/shard_map/ppermute | solution.py:26
  67.1 13.8 %collective-permute-start.4 = (f32[256,256]{1,0:T(8,128)}, f32[256,256]{1,0:T(8,128)}, u32[]{:S(2)}, u32[]{:S(2)}) collective-permute-start(f32[256,256]{1,0:T(8,128)} %get-tuple-element.27), channel_id=1, source_target_pairs={{0,1},{1,2},{2,3},{3,0},{4,5},{5,6},{6,7},{7,4},{8,9},{9,10},{10,1... | collective-permute-start | bytes 786440 | tf_op jit(solution)/shard_map/ppermute | solution.py:26
  73.1 31.6 %collective-permute-start.9 = (f32[2,256,256]{2,1,0:T(8,128)}, f32[2,256,256]{2,1,0:T(8,128)}, u32[]{:S(2)}, u32[]{:S(2)}) collective-permute-start(f32[2,256,256]{2,1,0:T(8,128)} %get-tuple-element.39), channel_id=1, source_target_pairs={{0,4},{4,8},{8,12},{12,0},{1,5},{5,9},{9,13},{13,1},{2,6},{6,10},{... | collective-permute-start | bytes 1572872 | tf_op jit(solution)/shard_map/ppermute | solution.py:26
  75.7 28.9 %collective-permute-start.10 = (f32[2,256,256]{2,1,0:T(8,128)}, f32[2,256,256]{2,1,0:T(8,128)}, u32[]{:S(2)}, u32[]{:S(2)}) collective-permute-start(f32[2,256,256]{2,1,0:T(8,128)} %get-tuple-element.40), channel_id=1, source_target_pairs={{0,12},{4,0},{8,4},{12,8},{1,13},{5,1},{9,5},{13,9},{2,14},{6,2},{... | collective-permute-start | bytes 1572872 | tf_op jit(solution)/shard_map/ppermute | solution.py:26
  80.9 18.1 %collective-permute-start.5 = (f32[256,256]{1,0:T(8,128)S(1)}, f32[256,256]{1,0:T(8,128)}, u32[]{:S(2)}, u32[]{:S(2)}) collective-permute-start(f32[256,256]{1,0:T(8,128)S(1)} %get-tuple-element.29), channel_id=1, source_target_pairs={{0,3},{1,0},{2,1},{3,2},{4,7},{5,4},{6,5},{7,6},{8,11},{9,8},{10,9... | collective-permute-start | bytes 786440 | tf_op jit(solution)/shard_map/ppermute | solution.py:26
  90.8 9.2 %copy-start.2 = (bf16[3,512,256]{2,1,0:T(8,128)(2,1)S(1)}, bf16[3,512,256]{2,1,0:T(8,128)(2,1)}, u32[]{:S(2)}) copy-start(bf16[3,512,256]{2,1,0:T(8,128)(2,1)} %copy-done.1) | copy-start | bytes 2359300
  90.8 9.3 %copy-start.4 = (bf16[3,512,256]{2,1,0:T(8,128)(2,1)S(1)}, bf16[3,512,256]{2,1,0:T(8,128)(2,1)}, u32[]{:S(2)}) copy-start(bf16[3,512,256]{2,1,0:T(8,128)(2,1)} %copy-done.3) | copy-start | bytes 2359300
  90.9 19.4 %collective-permute-start.7 = (f32[2,256,256]{2,1,0:T(8,128)}, f32[2,256,256]{2,1,0:T(8,128)S(1)}, u32[]{:S(2)}, u32[]{:S(2)}) collective-permute-start(f32[2,256,256]{2,1,0:T(8,128)} %collective-permute-done.2.refs_1_.refs_0_), channel_id=1, source_target_pairs={{0,4},{4,8},{8,12},{12,0},{1,5},{5,9},{9,13},{13,1},{2,6},{6,10},{... | collective-permute-start | bytes 1572872 | tf_op jit(solution)/shard_map/ppermute | solution.py:26
  93.1 17.2 %collective-permute-start.8 = (f32[2,256,256]{2,1,0:T(8,128)}, f32[2,256,256]{2,1,0:T(8,128)S(1)}, u32[]{:S(2)}, u32[]{:S(2)}) collective-permute-start(f32[2,256,256]{2,1,0:T(8,128)} %collective-permute-done.3.refs_4_.refs_3_), channel_id=1, source_target_pairs={{0,12},{4,0},{8,4},{12,8},{1,13},{5,1},{9,5},{13,9},{2,14},{6,2},{... | collective-permute-start | bytes 1572872 | tf_op jit(solution)/shard_map/ppermute | solution.py:26
  101.4 17.7 %collective-permute-start.6 = (f32[264,256]{1,0:T(8,128)S(1)}, f32[264,256]{1,0:T(8,128)S(1)}, u32[]{:S(2)}, u32[]{:S(2)}) collective-permute-start(f32[264,256]{1,0:T(8,128)S(1)} %shard_map.58), channel_id=1, source_target_pairs={{0,256},{16,272},{32,288},{48,304},{64,320},{80,336},{96,352},{112... | collective-permute-start | bytes 811016 | tf_op jit(solution)/shard_map/ppermute | solution.py:196
  107.7 16.7 %collective-permute-start.12 = (f32[256,512]{1,0:T(8,128)S(1)}, f32[256,512]{1,0:T(8,128)S(1)}, u32[]{:S(2)}, u32[]{:S(2)}) collective-permute-start(f32[256,512]{1,0:T(8,128)S(1)} %shard_map.61), channel_id=1, source_target_pairs={{0,256},{16,272},{32,288},{48,304},{64,320},{80,336},{96,352},{112... | collective-permute-start | bytes 1572872 | tf_op jit(solution)/shard_map/ppermute | solution.py:196
  111.7 17.1 %collective-permute-start.11 = (f32[256,256]{1,0:T(8,128)S(1)}, f32[256,256]{1,0:T(8,128)S(1)}, u32[]{:S(2)}, u32[]{:S(2)}) collective-permute-start(f32[256,256]{1,0:T(8,128)S(1)} %shard_map.59), channel_id=1, source_target_pairs={{0,256},{16,272},{32,288},{48,304},{64,320},{80,336},{96,352},{112... | collective-permute-start | bytes 786440 | tf_op jit(solution)/shard_map/ppermute | solution.py:196

commit v4 on v2

--- a/solution.py
+++ b/solution.py
@@ -58,7 +58,7 @@
 
 
 def window_kernel(groups, count, to_ref, *refs):
-    pieces, (high_ref, low_ref), extra = refs[:count], refs[count : count + 2], refs[count + 2 :]
+    pieces, (high_ref, low_ref) = refs[:count], refs[count:]
     for d in range(groups):
         per = count // groups
         j = 0
@@ -67,18 +67,29 @@
                 at = pl.ds(pl.multiple_of(to_ref[j] * BLK, BLK), BLK)
                 high_ref[d, at], low_ref[d, at] = halves(piece[pl.ds(i * BLK, BLK)])
                 j += 1
-    if extra:
-        first_ref, second_ref = extra
-        rows = first_ref.shape[0]
-        first_ref[...] = pieces[1][pl.ds(0, rows)]
-        second_ref[...] = pieces[2][pl.ds(rows, rows)]
-
-
-def split_window(to, groups, us, *pieces, forward=False):
+
+
+def halves_kernel(before_ref, after_ref, low_ref, high_ref):
+    rows = low_ref.shape[0]
+    low_ref[...] = before_ref[pl.ds(0, rows)]
+    high_ref[...] = after_ref[pl.ds(rows, rows)]
+
+
+def forward_halves(before, after):
+    out = jax.ShapeDtypeStruct((before.shape[0] // 2, before.shape[1]), F32)
+    return pl.pallas_call(
+        halves_kernel,
+        out_shape=[out, out],
+        in_specs=[VMEM] * 2,
+        out_specs=[VMEM] * 2,
+        compiler_params=pltpu.CompilerParams(vmem_limit_bytes=LIMIT),
+        cost_estimate=cost(0.3),
+    )(before, after)
+
+
+def split_window(to, groups, us, *pieces):
     rows, width = sum(p.shape[0] for p in pieces) // groups, pieces[0].shape[1]
     out = [jax.ShapeDtypeStruct((groups, rows, width), BF16)] * 2
-    if forward:
-        out += [jax.ShapeDtypeStruct((rows // 2, width), F32)] * 2
     return pl.pallas_call(
         functools.partial(window_kernel, groups, len(pieces)),
         out_shape=out,
@@ -204,9 +215,10 @@
     sources = jnp.sum(
         jnp.where(to[None, :] == jnp.arange(to.shape[0])[:, None], jnp.arange(to.shape[0])[None, :], 0), 1
     ).astype(jnp.int32)
-    *near, low, high = split_window(to, 3, 60, window, before, after, forward=True)
-    mine = after_all(mine, low)
+    low, high = forward_halves(before, after)
     far_low, far_high = shift(low, "col", 1), shift(high, "col", -1)
+    near = split_window(to, 3, 15, window, before, after)
+    mine = after_all(mine, *near)
     lower, upper_half = mine[: n_col // 2], mine[n_col // 2 :]
     b_low, a_high = shift(lower, "row", 1), shift(upper_half, "row", -1)
     b_high, a_low = shift(upper_half, "row", 1), shift(lower, "row", -1)

time: 127 us -> 127 us (level)
    unnamed x18 -> x20, local copies, waits for them, and re-layouts: 3.71 us -> 3.69 us
where the time goes in v4:
time: 127 us; the launch traced here: 126 us
  starting transfers between devices  65.1 us (51%)
  waiting for transfers between devices  37.1 us (29%)
  Pallas kernels  18.3 us (14%)
  local copies, waits for them, and re-layouts  4.92 us (4%)
    ppermute x10, starting transfers between devices, shift(): lax.ppermute(value, axis, [(i, (i + by) % size) for i in range(size)])  44.7 us
    ppermute x10, waiting for transfers between devices, shift(): lax.ppermute(value, axis, [(i, (i + by) % size) for i in range(size)])  22.1 us
    pallas_call x4, Pallas kernels, update(): pl.pallas_call(functools.partial(update_kernel, counts, firsts, more), ou...  9.93 us
    ppermute x3, starting transfers between devices, body(): to_sibling = lambda v: lax.ppermute(v, 'leaf', pairs)  8.99 us
    all_to_all x1, starting transfers between devices, body(): lax.all_to_all(by_row, 'col', 0, 0, tiled=True)  7.09 us
    all_to_all x1, waiting for transfers between devices, body(): by_row = lax.all_to_all(masked, 'row', 0, 0, tiled=True)  6.96 us
    ppermute x3, waiting for transfers between devices, body(): to_sibling = lambda v: lax.ppermute(v, 'leaf', pairs)  5.2 us
    all_to_all x1, starting transfers between devices, body(): by_row = lax.all_to_all(masked, 'row', 0, 0, tiled=True)  4.29 us
  transfers between devices with their start and end apart: 15, of which 6 were waited for; matrix products, arithmetic and copies ran while one was open for 1% of the time, Pallas kernels for 11%

profile of v4, /device:TPU:448, one launch (start us, length us, event | category | flops | bytes accessed | tf_op | source)
XLA Modules:
  0.0 126.4 jit_solution(13107960656991389276)
XLA Ops:
  0.0 0.0 copy-start.5
  0.0 1.2 copy-done.5
  1.2 0.0 copy-start.7
  1.2 0.7 copy-done.7
  1.9 1.6 %shard_map.55 = (f32[1024,256]{1,0:T(8,128)}, f32[512,256]{1,0:T(8,128)S(1)}) custom-call(s32[2,8]{1,0:T(2,128)S(1)} %bitcast.24, f32[1024,256]{1,0:T(8,128)S(1)} %copy-done.5), custom_call_target="tpu_custom_call" | custom-call | flops 1500000000 | bytes 3000000 | tf_op jit(solution)/shard_map/pallas_call | solution.py:41
  3.5 4.3 %all-to-all-start = ((f32[4,256,256]{2,1,0:T(8,128)}), f32[4,256,256]{2,1,0:T(8,128)}, u32[]{:S(2)}, u32[]{:S(2)}) async-start(f32[4,256,256]{2,1,0:T(8,128)} %bitcast.11), calls=%async_computation | async-start | bytes 2097152 | tf_op jit(solution)/shard_map/all_to_all | solution.py:210
  7.8 0.0 copy-start.8
  7.8 4.6 %collective-permute-start = (f32[512,256]{1,0:T(8,128)S(1)}, f32[512,256]{1,0:T(8,128)S(1)}, u32[]{:S(2)}, u32[]{:S(2)}) collective-permute-start(f32[512,256]{1,0:T(8,128)S(1)} %get-tuple-element.18.refs_0_), channel_id=1, source_target_pairs={{0,1},{1,2},{2,3},{3,0},{4,5},{5,6},{6,7},{7,4},{8,9},{9,10},{10,1... | collective-permute-start | bytes 1572872 | tf_op jit(solution)/shard_map/ppermute | solution.py:26
  12.4 3.6 %collective-permute-start.1 = (f32[512,256]{1,0:T(8,128)S(1)}, f32[512,256]{1,0:T(8,128)S(1)}, u32[]{:S(2)}, u32[]{:S(2)}) collective-permute-start(f32[512,256]{1,0:T(8,128)S(1)} %get-tuple-element.18.refs_0_), channel_id=1, source_target_pairs={{0,3},{1,0},{2,1},{3,2},{4,7},{5,4},{6,5},{7,6},{8,11},{9,8},{10,9... | collective-permute-start | bytes 1572872 | tf_op jit(solution)/shard_map/ppermute | solution.py:26
  16.1 0.1 broadcast_multiply_fusion
  16.2 0.1 iota_add_fusion
  16.3 7.0 %all-to-all-done = f32[4,256,256]{2,1,0:T(8,128)} async-done(((f32[4,256,256]{2,1,0:T(8,128)}), f32[4,256,256]{2,1,0:T(8,128)}, u32[]{:S(2)}, u32[]{:S(2)}) %all-to-all-start) | async-done | bytes 1048608 | tf_op jit(solution)/shard_map/all_to_all | solution.py:210
  23.2 7.1 %all-to-all-start.1 = ((f32[4,256,256]{2,1,0:T(8,128)}), f32[4,256,256]{2,1,0:T(8,128)S(1)}, u32[]{:S(2)}, u32[]{:S(2)}) async-start(f32[4,256,256]{2,1,0:T(8,128)} %all-to-all-done), calls=%async_computation.1 | async-start | bytes 2097152 | tf_op jit(solution)/shard_map/all_to_all | solution.py:211
  30.3 0.0 copy-done.8
  30.3 2.8 %collective-permute-done.refs_1_.before_ref = f32[512,256]{1,0:T(8,128)S(1)} collective-permute-done((f32[512,256]{1,0:T(8,128)S(1)}, f32[512,256]{1,0:T(8,128)S(1)}, u32[]{:S(2)}, u32[]{:S(2)}) %collective-permute-start) | collective-permute-done | bytes 524320 | tf_op jit(solution)/shard_map/ppermute | solution.py:26
  33.2 19.3 %collective-permute-done.1.refs_2_.after_ref = f32[512,256]{1,0:T(8,128)S(1)} collective-permute-done((f32[512,256]{1,0:T(8,128)S(1)}, f32[512,256]{1,0:T(8,128)S(1)}, u32[]{:S(2)}, u32[]{:S(2)}) %collective-permute-start.1) | collective-permute-done | bytes 524320 | tf_op jit(solution)/shard_map/ppermute | solution.py:26
  52.4 0.8 shard_map.57
  53.2 0.0 copy-start.6
  53.2 5.4 %collective-permute-start.4 = (f32[256,256]{1,0:T(8,128)}, f32[256,256]{1,0:T(8,128)S(1)}, u32[]{:S(2)}, u32[]{:S(2)}) collective-permute-start(f32[256,256]{1,0:T(8,128)} %get-tuple-element.24), channel_id=1, source_target_pairs={{0,1},{1,2},{2,3},{3,0},{4,5},{5,6},{6,7},{7,4},{8,9},{9,10},{10,1... | collective-permute-start | bytes 786440 | tf_op jit(solution)/shard_map/ppermute | solution.py:26
  58.6 0.7 shard_map.56
  59.4 0.0 copy-done.6
  59.4 0.0 copy-start.1
  59.4 0.9 copy-done.1
  60.3 0.9 copy-done.3
  61.2 2.8 %all-to-all-done.1.refs_1_.refs_0_ = f32[4,256,256]{2,1,0:T(8,128)S(1)} async-done(((f32[4,256,256]{2,1,0:T(8,128)}), f32[4,256,256]{2,1,0:T(8,128)S(1)}, u32[]{:S(2)}, u32[]{:S(2)}) %all-to-all-start.1) | async-done | bytes 1048608 | tf_op jit(solution)/shard_map/all_to_all | solution.py:211
  63.9 1.1 fusion.1
  65.0 3.1 %collective-permute-start.2 = (f32[2,256,256]{2,1,0:T(8,128)}, f32[2,256,256]{2,1,0:T(8,128)}, u32[]{:S(2)}, u32[]{:S(2)}) collective-permute-start(f32[2,256,256]{2,1,0:T(8,128)} %get-tuple-element.36), channel_id=1, source_target_pairs={{0,4},{4,8},{8,12},{12,0},{1,5},{5,9},{9,13},{13,1},{2,6},{6,10},{... | collective-permute-start | bytes 1572872 | tf_op jit(solution)/shard_map/ppermute | solution.py:26
  68.0 4.0 %collective-permute-start.3 = (f32[2,256,256]{2,1,0:T(8,128)}, f32[2,256,256]{2,1,0:T(8,128)}, u32[]{:S(2)}, u32[]{:S(2)}) collective-permute-start(f32[2,256,256]{2,1,0:T(8,128)} %get-tuple-element.35), channel_id=1, source_target_pairs={{0,12},{4,0},{8,4},{12,8},{1,13},{5,1},{9,5},{13,9},{2,14},{6,2},{... | collective-permute-start | bytes 1572872 | tf_op jit(solution)/shard_map/ppermute | solution.py:26
  72.1 0.1 select_reduce_fusion.2.from_ref
  72.2 1.9 %collective-permute-start.9 = (f32[2,256,256]{2,1,0:T(8,128)}, f32[2,256,256]{2,1,0:T(8,128)}, u32[]{:S(2)}, u32[]{:S(2)}) collective-permute-start(f32[2,256,256]{2,1,0:T(8,128)} %get-tuple-element.35), channel_id=1, source_target_pairs={{0,4},{4,8},{8,12},{12,0},{1,5},{5,9},{9,13},{13,1},{2,6},{6,10},{... | collective-permute-start | bytes 1572872 | tf_op jit(solution)/shard_map/ppermute | solution.py:26
  74.1 5.1 %collective-permute-start.10 = (f32[2,256,256]{2,1,0:T(8,128)}, f32[2,256,256]{2,1,0:T(8,128)}, u32[]{:S(2)}, u32[]{:S(2)}) collective-permute-start(f32[2,256,256]{2,1,0:T(8,128)} %get-tuple-element.36), channel_id=1, source_target_pairs={{0,12},{4,0},{8,4},{12,8},{1,13},{5,1},{9,5},{13,9},{2,14},{6,2},{... | collective-permute-start | bytes 1572872 | tf_op jit(solution)/shard_map/ppermute | solution.py:26
  79.2 0.1 pad_add_fusion.2.quarter_ref
  79.3 0.0 collective-permute-done.4.refs_0_
  79.3 9.8 %collective-permute-start.5 = (f32[256,256]{1,0:T(8,128)}, f32[256,256]{1,0:T(8,128)}, u32[]{:S(2)}, u32[]{:S(2)}) collective-permute-start(f32[256,256]{1,0:T(8,128)} %copy-done.6), channel_id=1, source_target_pairs={{0,3},{1,0},{2,1},{3,2},{4,7},{5,4},{6,5},{7,6},{8,11},{9,8},{10,9... | collective-permute-start | bytes 786440 | tf_op jit(solution)/shard_map/ppermute | solution.py:26
  89.1 0.1 pad_add_fusion.1.place_ref
  89.2 0.1 add.92
  89.3 0.0 copy-done.9
  89.3 0.0 collective-permute-done.2.refs_1_.refs_0_
  89.3 2.1 %collective-permute-start.7 = (f32[2,256,256]{2,1,0:T(8,128)}, f32[2,256,256]{2,1,0:T(8,128)S(1)}, u32[]{:S(2)}, u32[]{:S(2)}) collective-permute-start(f32[2,256,256]{2,1,0:T(8,128)} %collective-permute-done.2.refs_1_.refs_0_), channel_id=1, source_target_pairs={{0,4},{4,8},{8,12},{12,0},{1,5},{5,9},{9,13},{13,1},{2,6},{6,10},{... | collective-permute-start | bytes 1572872 | tf_op jit(solution)/shard_map/ppermute | solution.py:26
  91.4 0.0 collective-permute-done.3.refs_4_.refs_3_
  91.4 5.1 %collective-permute-start.8 = (f32[2,256,256]{2,1,0:T(8,128)}, f32[2,256,256]{2,1,0:T(8,128)S(1)}, u32[]{:S(2)}, u32[]{:S(2)}) collective-permute-start(f32[2,256,256]{2,1,0:T(8,128)} %collective-permute-done.3.refs_4_.refs_3_), channel_id=1, source_target_pairs={{0,12},{4,0},{8,4},{12,8},{1,13},{5,1},{9,5},{13,9},{2,14},{6,2},{... | collective-permute-start | bytes 1572872 | tf_op jit(solution)/shard_map/ppermute | solution.py:26
  96.6 0.0 collective-permute-done.5.refs_1_
  96.6 1.0 shard_map.58
  97.6 0.0 copy-done
  97.6 0.0 copy-done.2
  97.6 0.0 copy-done.4
  97.6 1.3 %shard_map.59 = f32[264,256]{1,0:T(8,128)S(1)} custom-call(s32[1]{0:T(128)} %bitcast.quarter_ref, s32[4]{0:T(128)S(1)} %select_reduce_fusion.2.from_ref, s32[4]{0:T(128)S(1)} %pad_add_fusion.1.place_ref, bf16[3,512,256]{2,1,0:T(8,128)(2,1)S(1)} %copy-done.2, bf16[3,512,256]{2,1,0:T(8,128)(2,1)S(1)} %copy-done.4, ...), custom_call_target="tpu_custom_call" | custom-call | flops 1000000000 | bytes 2000000 | tf_op jit(solution)/shard_map/pallas_call | solution.py:144
  99.0 3.1 %collective-permute-start.6 = (f32[264,256]{1,0:T(8,128)S(1)}, f32[264,256]{1,0:T(8,128)S(1)}, u32[]{:S(2)}, u32[]{:S(2)}) collective-permute-start(f32[264,256]{1,0:T(8,128)S(1)} %shard_map.59), channel_id=1, source_target_pairs={{0,256},{16,272},{32,288},{48,304},{64,320},{80,336},{96,352},{112... | collective-permute-start | bytes 811016 | tf_op jit(solution)/shard_map/ppermute | solution.py:207
  102.1 0.0 collective-permute-done.9.refs_2_.refs_1_
  102.1 0.0 collective-permute-done.10.refs_3_.refs_2_
  102.2 3.0 %shard_map.62 = f32[256,512]{1,0:T(8,128)S(1)} custom-call(s32[2]{0:T(128)S(1)} %pad_add_fusion.2.quarter_ref, s32[4]{0:T(128)S(1)} %select_reduce_fusion.2.from_ref, s32[4]{0:T(128)S(1)} %pad_add_fusion.1.place_ref, bf16[3,512,256]{2,1,0:T(8,128)(2,1)S(1)} %copy-done.2, bf16[3,512,256]{2,1,0:T(8,128)(2,1)S(1)} %copy-done.4, ...), custom_call_target="tpu_custom_call" | custom-call | flops 2000000000 | bytes 4000000 | tf_op jit(solution)/shard_map/pallas_call | solution.py:144
  105.1 2.7 %collective-permute-start.12 = (f32[256,512]{1,0:T(8,128)S(1)}, f32[256,512]{1,0:T(8,128)S(1)}, u32[]{:S(2)}, u32[]{:S(2)}) collective-permute-start(f32[256,512]{1,0:T(8,128)S(1)} %shard_map.62), channel_id=1, source_target_pairs={{0,256},{16,272},{32,288},{48,304},{64,320},{80,336},{96,352},{112... | collective-permute-start | bytes 1572872 | tf_op jit(solution)/shard_map/ppermute | solution.py:207
  107.8 0.0 collective-permute-done.7.refs_0_.refs_5_
  107.9 0.0 collective-permute-done.8.refs_1_.refs_6_
  107.9 1.4 %shard_map.60 = f32[256,256]{1,0:T(8,128)S(1)} custom-call(s32[1]{0:T(128)} %bitcast.3.quarter_ref, s32[4]{0:T(128)S(1)} %select_reduce_fusion.2.from_ref, s32[4]{0:T(128)S(1)} %pad_add_fusion.1.place_ref, bf16[3,512,256]{2,1,0:T(8,128)(2,1)S(1)} %copy-done.2, bf16[3,512,256]{2,1,0:T(8,128)(2,1)S(1)} %copy-done.4, ...), custom_call_target="tpu_custom_call" | custom-call | flops 1000000000 | bytes 2000000 | tf_op jit(solution)/shard_map/pallas_call | solution.py:144
  109.2 3.1 %collective-permute-start.11 = (f32[256,256]{1,0:T(8,128)S(1)}, f32[256,256]{1,0:T(8,128)S(1)}, u32[]{:S(2)}, u32[]{:S(2)}) collective-permute-start(f32[256,256]{1,0:T(8,128)S(1)} %shard_map.60), channel_id=1, source_target_pairs={{0,256},{16,272},{32,288},{48,304},{64,320},{80,336},{96,352},{112... | collective-permute-start | bytes 786440 | tf_op jit(solution)/shard_map/ppermute | solution.py:207
  112.4 4.2 %shard_map.61.refs_0_ = f32[256,1024]{1,0:T(8,128)S(1)} custom-call(s32[4]{0:T(128)S(1)} %get-tuple-element.28.quarter_ref, s32[4]{0:T(128)S(1)} %select_reduce_fusion.2.from_ref, s32[4]{0:T(128)S(1)} %pad_add_fusion.1.place_ref, bf16[3,512,256]{2,1,0:T(8,128)(2,1)S(1)} %copy-done.2, bf16[3,512,256]{2,1,0:T(8,128)(2,1)S(1)} %copy-done.4, ...), custom_call_target="tpu_custom_call" | custom-call | flops 4000000000 | bytes 8000000 | tf_op jit(solution)/shard_map/pallas_call | solution.py:144
  116.6 0.0 collective-permute-done.6.refs_1_
  116.7 0.2 select_reduce_fusion
  116.9 0.1 slice.24.slots_ref
  116.9 4.4 %collective-permute-done.12.refs_2_ = f32[256,512]{1,0:T(8,128)S(1)} collective-permute-done((f32[256,512]{1,0:T(8,128)S(1)}, f32[256,512]{1,0:T(8,128)S(1)}, u32[]{:S(2)}, u32[]{:S(2)}) %collective-permute-start.12) | collective-permute-done | bytes 524320 | tf_op jit(solution)/shard_map/ppermute | solution.py:207
  121.4 2.1 %shard_map.63.sum_ref = f32[256,1536]{1,0:T(8,128)} custom-call(s32[8]{0:T(128)S(1)} %get-tuple-element.31.mine_ref, s32[8]{0:T(128)S(1)} %get-tuple-element.32.other_ref, f32[256,1024]{1,0:T(8,128)S(1)} %shard_map.61.refs_0_, f32[264,256]{1,0:T(8,128)S(1)} %collective-permute-done.6.refs_1_, f32[256,512]{1,0:T(8,128)S(1)} %collective-permute-done.12.refs_2_), custom_call_target="tpu_custom_call" | custom-call | flops 2000000000 | bytes 4000000 | tf_op jit(solution)/shard_map/pallas_call | solution.py:168
  123.4 0.7 collective-permute-done.11.value_ref
  124.2 2.2 %shard_map.64 = f32[256,1536]{1,0:T(8,128)} custom-call(s32[2]{0:T(128)S(1)} %slice.24.slots_ref, f32[256,256]{1,0:T(8,128)S(1)} %collective-permute-done.11.value_ref, f32[256,1536]{1,0:T(8,128)} %shard_map.63.sum_ref), custom_call_target="tpu_custom_call", output_to_operand_aliasing={{}: (2, {})} | custom-call | flops 1000000000 | bytes 2000000 | tf_op jit(solution)/shard_map/pallas_call | solution.py:185
  (12 shorter events, 0.1 us)
Async XLA Ops:
  0.0 1.2 copy-start.5
  1.2 0.7 copy-start.7
  3.5 19.7 %all-to-all-start = ((f32[4,256,256]{2,1,0:T(8,128)}), f32[4,256,256]{2,1,0:T(8,128)}, u32[]{:S(2)}, u32[]{:S(2)}) async-start(f32[4,256,256]{2,1,0:T(8,128)} %bitcast.11), calls=%async_computation | async-start | bytes 2097152 | tf_op jit(solution)/shard_map/all_to_all | solution.py:210
  7.8 22.5 %copy-start.8 = (s32[1,4]{1,0:T(1,128)S(1)}, s32[1,4]{1,0:T(1,128)}, u32[]{:S(2)}) copy-start(s32[1,4]{1,0:T(1,128)} %param.8) | copy-start | bytes 52
  7.8 25.3 %collective-permute-start = (f32[512,256]{1,0:T(8,128)S(1)}, f32[512,256]{1,0:T(8,128)S(1)}, u32[]{:S(2)}, u32[]{:S(2)}) collective-permute-start(f32[512,256]{1,0:T(8,128)S(1)} %get-tuple-element.18.refs_0_), channel_id=1, source_target_pairs={{0,1},{1,2},{2,3},{3,0},{4,5},{5,6},{6,7},{7,4},{8,9},{9,10},{10,1... | collective-permute-start | bytes 1572872 | tf_op jit(solution)/shard_map/ppermute | solution.py:26
  12.4 40.0 %collective-permute-start.1 = (f32[512,256]{1,0:T(8,128)S(1)}, f32[512,256]{1,0:T(8,128)S(1)}, u32[]{:S(2)}, u32[]{:S(2)}) collective-permute-start(f32[512,256]{1,0:T(8,128)S(1)} %get-tuple-element.18.refs_0_), channel_id=1, source_target_pairs={{0,3},{1,0},{2,1},{3,2},{4,7},{5,4},{6,5},{7,6},{8,11},{9,8},{10,9... | collective-permute-start | bytes 1572872 | tf_op jit(solution)/shard_map/ppermute | solution.py:26
  23.2 40.7 %all-to-all-start.1 = ((f32[4,256,256]{2,1,0:T(8,128)}), f32[4,256,256]{2,1,0:T(8,128)S(1)}, u32[]{:S(2)}, u32[]{:S(2)}) async-start(f32[4,256,256]{2,1,0:T(8,128)} %all-to-all-done), calls=%async_computation.1 | async-start | bytes 2097152 | tf_op jit(solution)/shard_map/all_to_all | solution.py:211
  53.2 6.2 %copy-start.6 = (f32[256,256]{1,0:T(8,128)}, f32[256,256]{1,0:T(8,128)S(1)}, u32[]{:S(2)}) copy-start(f32[256,256]{1,0:T(8,128)S(1)} %get-tuple-element.25) | copy-start | bytes 786436
  53.2 26.1 %collective-permute-start.4 = (f32[256,256]{1,0:T(8,128)}, f32[256,256]{1,0:T(8,128)S(1)}, u32[]{:S(2)}, u32[]{:S(2)}) collective-permute-start(f32[256,256]{1,0:T(8,128)} %get-tuple-element.24), channel_id=1, source_target_pairs={{0,1},{1,2},{2,3},{3,0},{4,5},{5,6},{6,7},{7,4},{8,9},{9,10},{10,1... | collective-permute-start | bytes 786440 | tf_op jit(solution)/shard_map/ppermute | solution.py:26
  59.4 0.9 copy-start.1
  60.3 0.9 copy-start.3
  61.2 28.1 %copy-start.9 = (s32[1,12]{1,0:T(1,128)S(1)}, s32[1,12]{1,0:T(1,128)}, u32[]{:S(2)}) copy-start(s32[1,12]{1,0:T(1,128)} %param.9) | copy-start | bytes 148
  63.9 33.7 %copy-start = (f32[512,1024]{1,0:T(8,128)S(1)}, f32[512,1024]{1,0:T(8,128)}, u32[]{:S(2)}) copy-start(f32[512,1024]{1,0:T(8,128)} %front_ref.7) | copy-start | bytes 6291460
  65.0 24.3 %collective-permute-start.2 = (f32[2,256,256]{2,1,0:T(8,128)}, f32[2,256,256]{2,1,0:T(8,128)}, u32[]{:S(2)}, u32[]{:S(2)}) collective-permute-start(f32[2,256,256]{2,1,0:T(8,128)} %get-tuple-element.36), channel_id=1, source_target_pairs={{0,4},{4,8},{8,12},{12,0},{1,5},{5,9},{9,13},{13,1},{2,6},{6,10},{... | collective-permute-start | bytes 1572872 | tf_op jit(solution)/shard_map/ppermute | solution.py:26
  68.0 23.3 %collective-permute-start.3 = (f32[2,256,256]{2,1,0:T(8,128)}, f32[2,256,256]{2,1,0:T(8,128)}, u32[]{:S(2)}, u32[]{:S(2)}) collective-permute-start(f32[2,256,256]{2,1,0:T(8,128)} %get-tuple-element.35), channel_id=1, source_target_pairs={{0,12},{4,0},{8,4},{12,8},{1,13},{5,1},{9,5},{13,9},{2,14},{6,2},{... | collective-permute-start | bytes 1572872 | tf_op jit(solution)/shard_map/ppermute | solution.py:26
  72.2 30.0 %collective-permute-start.9 = (f32[2,256,256]{2,1,0:T(8,128)}, f32[2,256,256]{2,1,0:T(8,128)}, u32[]{:S(2)}, u32[]{:S(2)}) collective-permute-start(f32[2,256,256]{2,1,0:T(8,128)} %get-tuple-element.35), channel_id=1, source_target_pairs={{0,4},{4,8},{8,12},{12,0},{1,5},{5,9},{9,13},{13,1},{2,6},{6,10},{... | collective-permute-start | bytes 1572872 | tf_op jit(solution)/shard_map/ppermute | solution.py:26
  74.1 28.1 %collective-permute-start.10 = (f32[2,256,256]{2,1,0:T(8,128)}, f32[2,256,256]{2,1,0:T(8,128)}, u32[]{:S(2)}, u32[]{:S(2)}) collective-permute-start(f32[2,256,256]{2,1,0:T(8,128)} %get-tuple-element.36), channel_id=1, source_target_pairs={{0,12},{4,0},{8,4},{12,8},{1,13},{5,1},{9,5},{13,9},{2,14},{6,2},{... | collective-permute-start | bytes 1572872 | tf_op jit(solution)/shard_map/ppermute | solution.py:26
  79.3 17.2 %collective-permute-start.5 = (f32[256,256]{1,0:T(8,128)}, f32[256,256]{1,0:T(8,128)}, u32[]{:S(2)}, u32[]{:S(2)}) collective-permute-start(f32[256,256]{1,0:T(8,128)} %copy-done.6), channel_id=1, source_target_pairs={{0,3},{1,0},{2,1},{3,2},{4,7},{5,4},{6,5},{7,6},{8,11},{9,8},{10,9... | collective-permute-start | bytes 786440 | tf_op jit(solution)/shard_map/ppermute | solution.py:26
  89.3 8.3 %copy-start.2 = (bf16[3,512,256]{2,1,0:T(8,128)(2,1)S(1)}, bf16[3,512,256]{2,1,0:T(8,128)(2,1)}, u32[]{:S(2)}) copy-start(bf16[3,512,256]{2,1,0:T(8,128)(2,1)} %copy-done.1) | copy-start | bytes 2359300
  89.3 8.3 %copy-start.4 = (bf16[3,512,256]{2,1,0:T(8,128)(2,1)S(1)}, bf16[3,512,256]{2,1,0:T(8,128)(2,1)}, u32[]{:S(2)}) copy-start(bf16[3,512,256]{2,1,0:T(8,128)(2,1)} %copy-done.3) | copy-start | bytes 2359300
  89.3 18.5 %collective-permute-start.7 = (f32[2,256,256]{2,1,0:T(8,128)}, f32[2,256,256]{2,1,0:T(8,128)S(1)}, u32[]{:S(2)}, u32[]{:S(2)}) collective-permute-start(f32[2,256,256]{2,1,0:T(8,128)} %collective-permute-done.2.refs_1_.refs_0_), channel_id=1, source_target_pairs={{0,4},{4,8},{8,12},{12,0},{1,5},{5,9},{9,13},{13,1},{2,6},{6,10},{... | collective-permute-start | bytes 1572872 | tf_op jit(solution)/shard_map/ppermute | solution.py:26
  91.4 16.4 %collective-permute-start.8 = (f32[2,256,256]{2,1,0:T(8,128)}, f32[2,256,256]{2,1,0:T(8,128)S(1)}, u32[]{:S(2)}, u32[]{:S(2)}) collective-permute-start(f32[2,256,256]{2,1,0:T(8,128)} %collective-permute-done.3.refs_4_.refs_3_), channel_id=1, source_target_pairs={{0,12},{4,0},{8,4},{12,8},{1,13},{5,1},{9,5},{13,9},{2,14},{6,2},{... | collective-permute-start | bytes 1572872 | tf_op jit(solution)/shard_map/ppermute | solution.py:26
  99.0 17.7 %collective-permute-start.6 = (f32[264,256]{1,0:T(8,128)S(1)}, f32[264,256]{1,0:T(8,128)S(1)}, u32[]{:S(2)}, u32[]{:S(2)}) collective-permute-start(f32[264,256]{1,0:T(8,128)S(1)} %shard_map.59), channel_id=1, source_target_pairs={{0,256},{16,272},{32,288},{48,304},{64,320},{80,336},{96,352},{112... | collective-permute-start | bytes 811016 | tf_op jit(solution)/shard_map/ppermute | solution.py:207
  105.1 16.2 %collective-permute-start.12 = (f32[256,512]{1,0:T(8,128)S(1)}, f32[256,512]{1,0:T(8,128)S(1)}, u32[]{:S(2)}, u32[]{:S(2)}) collective-permute-start(f32[256,512]{1,0:T(8,128)S(1)} %shard_map.62), channel_id=1, source_target_pairs={{0,256},{16,272},{32,288},{48,304},{64,320},{80,336},{96,352},{112... | collective-permute-start | bytes 1572872 | tf_op jit(solution)/shard_map/ppermute | solution.py:207
  109.2 15.0 %collective-permute-start.11 = (f32[256,256]{1,0:T(8,128)S(1)}, f32[256,256]{1,0:T(8,128)S(1)}, u32[]{:S(2)}, u32[]{:S(2)}) collective-permute-start(f32[256,256]{1,0:T(8,128)S(1)} %shard_map.60), channel_id=1, source_target_pairs={{0,256},{16,272},{32,288},{48,304},{64,320},{80,336},{96,352},{112... | collective-permute-start | bytes 786440 | tf_op jit(solution)/shard_map/ppermute | solution.py:207
